TPU v7x, 512 devices: a whole 4x8x8 slice. The times are simulated.
512 devices in a mesh: base: 32 (over y, x), chan: 16 (over z, core).
Axes of the slice: x: 4, y: 8, z: 8, core: 2. Of those that a mesh axis runs over, the one named last changes fastest.
Arguments:
- gains: float32 [128, 8, 2048], P('base', None, 'chan'), may hold values from -6 to 6
- delays: float32 [128, 2], P('base'), may hold values from -4 to 4
- model: bfloat16 [8192, 8, 2048], P('base', None, 'chan'), may hold values from -6 to 6
- antenna1: int32 [8192], P('base'), may hold values from 0 to 126, as said below
- antenna2: int32 [8192], P('base'), may hold values from 1 to 127, as said below
- dir_band: float32 [128, 8, 2048], P('base', None, 'chan'), may hold values from -6 to 6
- dir_delay: float32 [128, 2], P('base'), may hold values from -6 to 6
- res_band: float32 [128, 8, 2048], P('base', None, 'chan'), may hold values from -6 to 6
- res_delay: float32 [128, 2], P('base'), may hold values from -6 to 6
- iter_band: float32 [128, 8, 2048], P('base', None, 'chan'), may hold values from -6 to 6
- iter_delay: float32 [128, 2], P('base'), may hold values from -6 to 6
Outputs:
- new_iter_band: float32 [128, 8, 2048], P('base', None, 'chan')
- new_iter_delay: float32 [128, 2], P('base')
- new_res_band: float32 [128, 8, 2048], P('base', None, 'chan')
- new_res_delay: float32 [128, 2], P('base')
- new_dir_band: float32 [128, 8, 2048], P('base', None, 'chan')
- new_dir_delay: float32 [128, 2], P('base')
Inputs may be any that keep to these rules, and one draw needn't show every extreme that they name: antenna1[b] < antenna2[b]. Stations are in blocks of 4 consecutive numbers; the baselines in rows d * 256 to (d + 1) * 256 - 1 have one station in block d and the other in block d, d + 1, d - 1 or d plus half the number of blocks (modulo the number of blocks). `antenna2`: as for antenna1.
All inputs are finite; a program needn't handle non-finite values.
Results may differ from a plain program's by a relative error of at most 0.0003.
Values sent between devices are 32-bit elements; how exact they have to be, the bound alone decides.
No kernel may reach another device: no remote copies, remote signals or barrier semaphores. Data moves between devices by JAX's collectives and lax.ppermute only.
A program may use at most 64 MiB of HBM per device.

v0:
```python
import math

import jax
import jax.numpy as jnp
from jax import lax
from jax.sharding import PartitionSpec as P

full_turn = 2.0 * math.pi
damping_weight = 0.5


def split_parts(packed):
    count = packed.shape[0]
    width = packed.shape[-1]
    return (packed[:, :4].reshape(count, 2, 2, width), packed[:, 4:].reshape(count, 2, 2, width))


def join_parts(real, imag):
    count = real.shape[0]
    width = real.shape[-1]
    return jnp.concatenate([real.reshape(count, 4, width), imag.reshape(count, 4, width)], axis=1)


def matrix_product(left, right):
    return (
        left[:, :, 0:1, :] * right[:, None, 0, :, :] + left[:, :, 1:2, :] * right[:, None, 1, :, :]
    )


def complex_product(left, right):
    real = matrix_product(left[0], right[0]) - matrix_product(left[1], right[1])
    imag = matrix_product(left[0], right[1]) + matrix_product(left[1], right[0])
    return (real, imag)


def adjoint(pair):
    return (jnp.swapaxes(pair[0], 1, 2), -jnp.swapaxes(pair[1], 1, 2))


def station_terms(gains, delays, dir_band, dir_delay, freq, delay_scale):
    phase = full_turn * delays[:, :, None] * freq[None, None, :]
    cosine = jnp.cos(phase)[:, None, :, :]
    sine = jnp.sin(phase)[:, None, :, :]
    gain_re, gain_im = split_parts(gains)
    jones_re = cosine * gain_re - sine * gain_im
    jones_im = cosine * gain_im + sine * gain_re
    move_re, move_im = split_parts(dir_band)
    turned_re = cosine * move_re - sine * move_im
    turned_im = cosine * move_im + sine * move_re
    rate = full_turn * delay_scale * dir_delay[:, :, None] * freq[None, None, :]
    rate = rate[:, None, :, :]
    tangent_re = turned_re - rate * jones_im
    tangent_im = turned_im + rate * jones_re
    return (join_parts(jones_re, jones_im), join_parts(tangent_re, tangent_im), cosine, sine)


def baseline_change(jones_p, tangent_p, jones_q, tangent_q, model, multiplier_factor):
    model_pair = split_parts(model)
    right_q = complex_product(model_pair, adjoint(split_parts(jones_q)))
    left_p = complex_product(split_parts(jones_p), model_pair)
    first = complex_product(split_parts(tangent_p), right_q)
    second = complex_product(left_p, adjoint(split_parts(tangent_q)))
    change = join_parts(
        multiplier_factor * (first[0] + second[0]), multiplier_factor * (first[1] + second[1])
    )
    return (change, right_q, left_p)


def selector(labels_from, count):
    labels = jnp.arange(count, dtype=jnp.int32)
    return (labels_from[:, None] == labels[None, :]).astype(jnp.float32)


def body(
    gains,
    delays,
    model,
    antenna1,
    antenna2,
    dir_band,
    dir_delay,
    res_band,
    res_delay,
    iter_band,
    iter_delay,
):
    owned = gains.shape[0]
    width = gains.shape[2]
    baseline_rows = model.shape[0]
    chan_count = lax.axis_size("chan")
    stations = owned * lax.axis_size("base")
    channels = width * chan_count
    multiplier_factor = (owned / (2.0 * baseline_rows)) ** 0.5
    delay_scale = channels ** (-0.5)
    freq = (
        (lax.axis_index("chan") * width + jnp.arange(width, dtype=jnp.int32)).astype(jnp.float32)
        + 0.5
    ) / channels - 0.5
    jones, tangent, cosine, sine = station_terms(
        gains, delays, dir_band, dir_delay, freq, delay_scale
    )
    highest = lax.Precision.HIGHEST
    all_jones, all_tangent = (
        lax.all_gather(jones, "base", axis=0, tiled=True),
        lax.all_gather(tangent, "base", axis=0, tiled=True),
    )
    jones_p = jnp.take(all_jones, antenna1, axis=0)
    tangent_p = jnp.take(all_tangent, antenna1, axis=0)
    jones_q = jnp.take(all_jones, antenna2, axis=0)
    tangent_q = jnp.take(all_tangent, antenna2, axis=0)
    change, right_q, left_p = baseline_change(
        jones_p, tangent_p, jones_q, tangent_q, model.astype(jnp.float32), multiplier_factor
    )
    change_pair = split_parts(change)
    toward_p = complex_product(change_pair, adjoint(right_q))
    toward_q = complex_product(adjoint(change_pair), left_p)
    grad_p = join_parts(multiplier_factor * toward_p[0], multiplier_factor * toward_p[1]).reshape(
        baseline_rows, 8 * width
    )
    grad_q = join_parts(multiplier_factor * toward_q[0], multiplier_factor * toward_q[1]).reshape(
        baseline_rows, 8 * width
    )
    pick_both = jnp.concatenate(
        [selector(antenna1, stations), selector(antenna2, stations)], axis=0
    )
    stacked = jnp.concatenate([grad_p, grad_q], axis=0)
    station_grad = lax.dot_general(pick_both, stacked, (((0,), (0,)), ((), ())), precision=highest)
    owned_grad = lax.psum_scatter(
        station_grad.reshape(stations, 8, width), "base", scatter_dimension=0, tiled=True
    )
    grad_re, grad_im = split_parts(owned_grad)
    band_re = cosine * grad_re + sine * grad_im
    band_im = cosine * grad_im - sine * grad_re
    grad_band = join_parts(band_re, band_im)
    jones_re, jones_im = split_parts(jones)
    weight = full_turn * delay_scale * freq
    delay_part = jnp.sum(
        weight[None, None, :] * jnp.sum(jones_re * grad_im - jones_im * grad_re, axis=1), axis=-1
    )
    delay_sum = lax.psum(delay_part, "chan")
    curv_band = grad_band + damping_weight * dir_band
    curv_delay = delay_sum + damping_weight * dir_delay
    squares_local = jnp.sum(res_band * res_band) + jnp.sum(res_delay * res_delay) / chan_count
    curvature_local = jnp.sum(dir_band * curv_band) + jnp.sum(dir_delay * curv_delay) / chan_count
    squares = lax.psum(squares_local, ("base", "chan"))
    curvature = lax.psum(curvature_local, ("base", "chan"))
    alpha = squares / curvature
    new_iter_band = iter_band + alpha * dir_band
    new_iter_delay = iter_delay + alpha * dir_delay
    new_res_band = res_band - alpha * curv_band
    new_res_delay = res_delay - alpha * curv_delay
    fresh_local = (
        jnp.sum(new_res_band * new_res_band) + jnp.sum(new_res_delay * new_res_delay) / chan_count
    )
    fresh = lax.psum(fresh_local, ("base", "chan"))
    ratio = fresh / squares
    new_dir_band = new_res_band + ratio * dir_band
    new_dir_delay = new_res_delay + ratio * dir_delay
    return (new_iter_band, new_iter_delay, new_res_band, new_res_delay, new_dir_band, new_dir_delay)


def solution(mesh):
    in_specs = (
        P("base", None, "chan"),
        P("base", None),
        P("base", None, "chan"),
        P("base"),
        P("base"),
        P("base", None, "chan"),
        P("base", None),
        P("base", None, "chan"),
        P("base", None),
        P("base", None, "chan"),
        P("base", None),
    )
    out_specs = (
        P("base", None, "chan"),
        P("base", None),
        P("base", None, "chan"),
        P("base", None),
        P("base", None, "chan"),
        P("base", None),
    )
    return jax.shard_map(body, mesh=mesh, in_specs=in_specs, out_specs=out_specs, check_vma=False)
```

profile of v0, /device:TPU:1, one launch (start us, length us, event | category | flops | bytes accessed | tf_op | source)
XLA Modules:
  0.0 594.3 jit_solution(6797502081238301903)
XLA Ops:
  7.2 0.7 compare_select_fusion
  7.9 0.7 compare_and_fusion
  8.6 0.7 broadcast_multiply_fusion.2
  9.4 0.7 broadcast_multiply_fusion.1
  10.3 0.8 multiply_add_fusion.3
  11.2 39.9 %all_gather.7 = f32[128,8,128]{2,1,0:T(8,128)S(1)} all-gather(f32[4,8,128]{2,1,0:T(8,128)S(1)} %pad_maximum_fusion.3), channel_id=1, replica_groups=mesh['base'=32,'chan'=16] {'base'}, dimensions={0}, use_global_device_ids=true | all-gather | bytes 540672 | tf_op jit(solution)/shard_map/all_gather | solution.py:104
  51.1 35.7 %all_gather.6 = f32[128,8,128]{2,1,0:T(8,128)S(1)} all-gather(f32[4,8,128]{2,1,0:T(8,128)S(1)} %pad_maximum_fusion.2), channel_id=1, replica_groups=mesh['base'=32,'chan'=16] {'base'}, dimensions={0}, use_global_device_ids=true | all-gather | bytes 540672 | tf_op jit(solution)/shard_map/all_gather | solution.py:105
  86.8 1.0 gather_fusion.1
  87.9 1.0 gather_fusion.3
  88.9 2.0 gather_fusion
  91.0 2.0 gather_fusion.2
  93.1 0.4 fusion.23
  93.6 0.4 fusion.25
  94.4 0.8 copy-done
  96.5 0.4 fusion.33
  97.0 1.2 add_subtract_fusion.1
  98.1 0.4 fusion.27
  98.6 0.4 fusion.29
  100.0 0.4 fusion.24
  100.4 0.4 fusion.26
  101.0 1.1 add_subtract_fusion
  102.2 1.0 add_subtract_fusion.2
  104.4 0.4 fusion.21
  104.8 0.4 fusion.22
  105.4 0.4 fusion.28
  105.8 0.4 fusion.30
  106.2 5.1 add_multiply_fusion.4
  111.4 0.4 fusion.17
  111.8 0.4 fusion.18
  112.2 1.1 subtract_multiply_fusion.1
  113.8 0.4 fusion.19
  114.2 0.4 fusion.20
  114.6 1.4 subtract_multiply_fusion
  116.4 0.9 fusion.4
  117.4 0.9 copy.131
  118.3 0.6 multiply_reduce_fusion.5
  119.6 0.6 multiply_reduce_fusion.2
  120.2 236.9 %reduce-scatter.2.cloned.1.call-done = f32[4,8,128]{2,1,0:T(8,128)} async-done(((f32[128,8,128]{2,1,0:T(8,128)}), f32[4,8,128]{2,1,0:T(8,128)}) %reduce-scatter.2.cloned.1.call-update) | async-done | bytes 16400 | tf_op jit(solution)/shard_map/reduce_scatter | solution.py:128
  357.1 0.8 multiply_add_fusion.2
  358.7 29.9 %psum.29 = f32[4,2]{0,1:T(2,128)S(1)} all-reduce(f32[4,2]{0,1:T(2,128)S(1)} %fusion.10), channel_id=1, replica_groups=mesh['base'=32,'chan'=16] {'chan'}, use_global_device_ids=true, to_apply=%region_7.9 | all-reduce | flops 8 | bytes 64 | tf_op jit(solution)/shard_map/psum | solution.py:140
  388.5 0.6 multiply_reduce_fusion.4
  389.8 0.6 multiply_reduce_fusion.1
  391.1 95.2 %all-reduce = (f32[]{:T(128)}, f32[]{:T(128)}) all-reduce(f32[]{:T(128)S(6)} %add.260, f32[]{:T(128)S(6)} %add.320), channel_id=1, replica_groups=mesh['base'=32,'chan'=16] {'base','chan'}, use_global_device_ids=true, to_apply=%region_2.3 | all-reduce | flops 2 | bytes 16 | tf_op jit(solution)/shard_map/psum | solution.py:145
  487.6 0.6 multiply_reduce_fusion.3
  488.3 0.6 multiply_reduce_fusion
  490.2 94.8 %psum.31 = f32[]{:T(128)} all-reduce(f32[]{:T(128)S(6)} %add.323), channel_id=1, replica_groups=mesh['base'=32,'chan'=16] {'base','chan'}, use_global_device_ids=true, to_apply=%region_12.14 | all-reduce | flops 1 | bytes 8 | tf_op jit(solution)/shard_map/psum | solution.py:155
  586.3 0.6 multiply_add_fusion.5
  586.9 0.6 multiply_add_fusion
  (78 shorter events, 5.7 us)
Async XLA Ops:
  7.2 349.9 %reduce-scatter.2.cloned.1.call-start = ((), (), s32[]{:S(2)}) async-start(), calls=%async_computation.1 | async-start | bytes 540672 | tf_op jit(solution)/shard_map/reduce_scatter | solution.py:128
  87.9 1.0 copy-start.8
  91.0 2.0 copy-start.2
  94.0 1.2 copy-start
  94.0 1.5 copy-start.1
  98.6 0.7 copy-start.9
  117.3 1.0 copy-start.11
  117.3 2.2 copy-start.4
  117.3 271.2 %copy-start.6 = (f32[4,2]{0,1:T(2,128)S(1)}, f32[4,2]{0,1:T(2,128)}, u32[]{:S(2)}) copy-start(f32[4,2]{0,1:T(2,128)} %param.19) | copy-start | bytes 100
  117.3 272.5 %copy-start.3 = (f32[4,8,128]{2,1,0:T(8,128)S(1)}, f32[4,8,128]{2,1,0:T(8,128)}, u32[]{:S(2)}) copy-start(f32[4,8,128]{2,1,0:T(8,128)} %param.18) | copy-start | bytes 49156
  117.3 468.9 %copy-start.12 = (f32[4,2]{0,1:T(2,128)S(1)}, f32[4,2]{0,1:T(2,128)}, u32[]{:S(2)}) copy-start(f32[4,2]{0,1:T(2,128)} %param.23) | copy-start | bytes 100
  117.4 469.5 %copy-start.7 = (f32[4,8,128]{2,1,0:T(8,128)S(1)}, f32[4,8,128]{2,1,0:T(8,128)}, u32[]{:S(2)}) copy-start(f32[4,8,128]{2,1,0:T(8,128)} %param.22) | copy-start | bytes 49156
  488.3 99.2 %copy-start.10 = (f32[4,2]{0,1:T(2,128)}, f32[4,2]{0,1:T(2,128)S(1)}, u32[]{:S(2)}) copy-start(f32[4,2]{0,1:T(2,128)S(1)} %get-tuple-element.10) | copy-start | bytes 100
  488.9 98.6 %copy-start.5 = (f32[4,8,128]{2,1,0:T(8,128)}, f32[4,8,128]{2,1,0:T(8,128)S(1)}, u32[]{:S(2)}) copy-start(f32[4,8,128]{2,1,0:T(8,128)S(1)} %get-tuple-element.12) | copy-start | bytes 49156
Sparse Core Ops, SparseCore 0:
  118.4 238.6 reduce-scatter.1
where the time goes:
time: 595 us; the launch traced here: 594 us
  blocking collectives  296 us (50%)
  waiting for transfers between devices  237 us (40%)
  other arithmetic  22 us (4%)
  between operations  21.3 us (4%)
  local copies, waits for them, and re-layouts  17.6 us (3%)
    reduce_scatter x1, waiting for transfers between devices, body(): lax.psum_scatter(station_grad.reshape(stations, 8, width), 'base', scatte...  237 us
    psum x1, blocking collectives, body(): squares = lax.psum(squares_local, ('base', 'chan'))  95.2 us
    psum x1, blocking collectives, body(): fresh = lax.psum(fresh_local, ('base', 'chan'))  94.8 us
    all_gather x1, blocking collectives, body(): lax.all_gather(jones, 'base', axis=0, tiled=True)  39.9 us
    all_gather x1, blocking collectives, body(): lax.all_gather(tangent, 'base', axis=0, tiled=True)  35.7 us
    psum x1, blocking collectives, body(): delay_sum = lax.psum(delay_part, 'chan')  29.9 us
  transfers between devices with their start and end apart: 1, of which 1 were waited for; matrix products, arithmetic and copies ran while one was open for 0% of the time, Pallas kernels for 0%

commit v1 on v0

v1 whole, which is shorter than its diff:
```python
import math

import jax
import jax.numpy as jnp
from jax import lax
from jax.experimental import pallas as pl
from jax.experimental.pallas import tpu as pltpu
from jax.sharding import Mesh
from jax.sharding import PartitionSpec as P

full_turn = 2.0 * math.pi
damping_weight = 0.5

f32 = jnp.float32
bf16 = jnp.bfloat16


def vmem():
    return pl.BlockSpec(memory_space=pltpu.VMEM)


def smem():
    return pl.BlockSpec(memory_space=pltpu.SMEM)


def params(mib):
    return pltpu.CompilerParams(vmem_limit_bytes=mib * 1024 * 1024)


def shape(*dims, dtype=f32):
    return jax.ShapeDtypeStruct(dims, dtype)


def frequencies(chan, width, channels):
    index = lax.broadcasted_iota(jnp.int32, (1, width), 1) + chan * width
    return (index.astype(f32) + 0.5) / channels - 0.5


def column(row_ref):
    count = row_ref.shape[1]
    eye = lax.broadcasted_iota(jnp.int32, (count, count), 0) == lax.broadcasted_iota(
        jnp.int32, (count, count), 1
    )
    parts = [
        jnp.sum(
            jnp.where(eye, jnp.broadcast_to(row_ref[a : a + 1, :], (count, count)), 0.0),
            axis=1,
            keepdims=True,
        )
        for a in range(2)
    ]
    return jnp.concatenate(parts, axis=0)


def station_kernel(
    chan_ref, gains_ref, band_ref, delays_ref, move_ref, terms_ref, turn_ref, packed, *, channels
):
    owned, _, width = gains_ref.shape
    half = 2 * owned
    delay_scale = channels ** (-0.5)
    freq = frequencies(chan_ref[0], width, channels)
    phase = full_turn * column(delays_ref) * freq
    rate = full_turn * delay_scale * column(move_ref) * freq
    cosine = jnp.cos(phase)
    sine = jnp.sin(phase)
    turn_ref[0:half, :] = cosine
    turn_ref[half : 2 * half, :] = sine
    for j in range(8):
        packed[j * owned : (j + 1) * owned, :] = gains_ref[:, j, :]
        packed[(8 + j) * owned : (9 + j) * owned, :] = band_ref[:, j, :]
    for r in range(2):
        re = slice(r * half, (r + 1) * half)
        im = slice((2 + r) * half, (3 + r) * half)
        move_re = slice((4 + r) * half, (5 + r) * half)
        move_im = slice((6 + r) * half, (7 + r) * half)
        jones_re = cosine * packed[re, :] - sine * packed[im, :]
        jones_im = cosine * packed[im, :] + sine * packed[re, :]
        terms_ref[re, :] = jones_re
        terms_ref[im, :] = jones_im
        terms_ref[move_re, :] = (
            cosine * packed[move_re, :] - sine * packed[move_im, :] - rate * jones_im
        )
        terms_ref[move_im, :] = (
            cosine * packed[move_im, :] + sine * packed[move_re, :] + rate * jones_re
        )


def prepare_kernel(block_ref, model_ref, first_ref, second_ref, model_out, gather_out, scatter_out, *, owned, blocks):
    rows = first_ref.shape[1]
    width = model_ref.shape[1]
    group = 32
    block = block_ref[0]
    size = 8 * group
    out_row = lax.broadcasted_iota(jnp.int32, (size, size), 0)
    in_row = lax.broadcasted_iota(jnp.int32, (size, size), 1)
    wanted = (out_row % group) * 8 + out_row // group
    shuffle = jnp.where(in_row == wanted, 1.0, 0.0).astype(bf16)
    for g in range(rows // group):
        part = jnp.dot(
            shuffle, model_ref[g * size : (g + 1) * size, :], preferred_element_type=f32
        )
        for j in range(8):
            model_out[j, g * group : (g + 1) * group, :] = part[j * group : (j + 1) * group, :]
    slots = 4 * owned
    slot = lax.broadcasted_iota(jnp.int32, (slots, 2 * rows), 0)
    kind = slot // owned
    offset = jnp.where(kind == 0, 0, jnp.where(kind == 1, 1, jnp.where(kind == 2, blocks - 1, blocks // 2)))
    station = ((block + offset) % blocks) * owned + slot % owned
    both = jnp.concatenate([first_ref[...], second_ref[...]], axis=1)
    pick = jnp.where(station == both, 1.0, 0.0)
    scatter_out[...] = pick.astype(bf16)
    filled = jnp.concatenate([pick] * 3 + [jnp.zeros((128 - 3 * slots, 2 * rows), f32)], axis=0)
    gather_out[...] = jnp.transpose(filled).astype(bf16)


def times(a, b):
    out = []
    for r in range(2):
        for c in range(2):
            out.append(
                a[r * 2] * b[c] - a[4 + r * 2] * b[4 + c] + a[r * 2 + 1] * b[2 + c] - a[5 + r * 2] * b[6 + c]
            )
    for r in range(2):
        for c in range(2):
            out.append(
                a[r * 2] * b[4 + c] + a[4 + r * 2] * b[c] + a[r * 2 + 1] * b[6 + c] + a[5 + r * 2] * b[2 + c]
            )
    return out


def times_adjoint(a, b):
    out = []
    for r in range(2):
        for c in range(2):
            out.append(
                a[r * 2] * b[c * 2]
                + a[4 + r * 2] * b[4 + c * 2]
                + a[r * 2 + 1] * b[c * 2 + 1]
                + a[5 + r * 2] * b[5 + c * 2]
            )
    for r in range(2):
        for c in range(2):
            out.append(
                a[4 + r * 2] * b[c * 2]
                - a[r * 2] * b[4 + c * 2]
                + a[5 + r * 2] * b[c * 2 + 1]
                - a[r * 2 + 1] * b[5 + c * 2]
            )
    return out


def adjoint_times(a, b):
    out = []
    for r in range(2):
        for c in range(2):
            out.append(
                a[r] * b[c] + a[4 + r] * b[4 + c] + a[2 + r] * b[2 + c] + a[6 + r] * b[6 + c]
            )
    for r in range(2):
        for c in range(2):
            out.append(
                a[r] * b[4 + c] - a[4 + r] * b[c] + a[2 + r] * b[6 + c] - a[6 + r] * b[2 + c]
            )
    return out


def baseline_kernel(
    own_ref, next_ref, last_ref, far_ref, model_ref, gather_ref, scatter_ref,
    own_out, next_out, last_out, far_out, table, picked, grads, *, factor
):
    _, rows, width = model_ref.shape
    slots = table.shape[0]
    owned = slots // 4
    for k, ref in enumerate((own_ref, next_ref, last_ref, far_ref)):
        for j in range(16):
            table[k * owned : (k + 1) * owned, j * width : (j + 1) * width] = ref[
                j * owned : (j + 1) * owned, :
            ]
    exact = table[...]
    high = exact.astype(bf16)
    rest = exact - high.astype(f32)
    middle = rest.astype(bf16)
    low = (rest - middle.astype(f32)).astype(bf16)
    split = jnp.concatenate(
        [high, middle, low, jnp.zeros((128 - 3 * slots, exact.shape[1]), bf16)], axis=0
    )
    pick = gather_ref[...]
    step = 2 * width
    for n in range(0, 16 * width, step):
        picked[:, n : n + step] = jnp.dot(pick, split[:, n : n + step], preferred_element_type=f32)

    def chunk(i, carry):
        at = pl.ds(pl.multiple_of(i * 8, 8), 8)
        at_q = pl.ds(pl.multiple_of(rows + i * 8, 8), 8)
        cols = [slice(j * width, (j + 1) * width) for j in range(16)]
        model = [model_ref[j, at, :] for j in range(8)]
        right = times_adjoint(model, [picked[at_q, c] for c in cols[:8]])
        left = times([picked[at, c] for c in cols[:8]], model)
        one = times([picked[at, c] for c in cols[8:]], right)
        two = times_adjoint(left, [picked[at_q, c] for c in cols[8:]])
        change = [a + b for a, b in zip(one, two)]
        for c, value in zip(cols, times_adjoint(change, right)):
            grads[at, c] = value
        for c, value in zip(cols, adjoint_times(change, left)):
            grads[at_q, c] = value
        return carry

    lax.fori_loop(0, rows // 8, chunk, 0, unroll=2)
    sums = []
    for n in range(0, 8 * width, step):
        value = grads[:, n : n + step]
        high = value.astype(bf16)
        low = (value - high.astype(f32)).astype(bf16)
        total = jnp.dot(scatter_ref[...], high, preferred_element_type=f32) + jnp.dot(
            scatter_ref[...], low, preferred_element_type=f32
        )
        table[:, n : n + step] = factor * total
    for k, ref in enumerate((own_out, next_out, last_out, far_out)):
        for j in range(8):
            ref[j * owned : (j + 1) * owned, :] = table[
                k * owned : (k + 1) * owned, j * width : (j + 1) * width
            ]


def curvature_kernel(
    place_ref, own_ref, a_ref, b_ref, c_ref, terms_ref, turn_ref, band_ref, res_ref, delay_ref, res_delay_ref,
    curv_ref, row_ref, *, channels
):
    owned, _, width = band_ref.shape
    half = 2 * owned
    delay_scale = channels ** (-0.5)
    freq = frequencies(place_ref[0], width, channels)
    cosine = turn_ref[0:half, :]
    sine = turn_ref[half : 2 * half, :]
    total = own_ref[...] + a_ref[...] + b_ref[...] + c_ref[...]
    moved = jnp.zeros((half, width), f32)
    for r in range(2):
        re = slice(r * half, (r + 1) * half)
        im = slice((2 + r) * half, (3 + r) * half)
        grad_re, grad_im = total[re, :], total[im, :]
        moved = moved + (terms_ref[re, :] * grad_im - terms_ref[im, :] * grad_re)
        band_re = cosine * grad_re + sine * grad_im
        band_im = cosine * grad_im - sine * grad_re
        for a in range(2):
            rows = slice(a * owned, (a + 1) * owned)
            j = 2 * r + a
            curv_ref[:, j, :] = band_re[rows, :] + damping_weight * band_ref[:, j, :]
            curv_ref[:, 4 + j, :] = band_im[rows, :] + damping_weight * band_ref[:, 4 + j, :]
    moved = jnp.sum(moved * (full_turn * delay_scale * freq), axis=1, keepdims=True)
    curv, band, res = curv_ref[...], band_ref[...], res_ref[...]
    scalars = [
        jnp.sum(jnp.sum(jnp.sum(x, axis=0), axis=0, keepdims=True), axis=1, keepdims=True)
        for x in (res * res, res * curv, curv * curv, band * curv)
    ]
    here = jnp.where(place_ref[1] == 0, 1.0, 0.0)
    values = jnp.concatenate(
        [moved] + scalars + [jnp.zeros((4, 1), f32)]
        + [here * column(delay_ref), here * column(res_delay_ref)],
        axis=0,
    )
    count = values.shape[0]
    diagonal = lax.broadcasted_iota(jnp.int32, (count, width), 0) == lax.broadcasted_iota(
        jnp.int32, (count, width), 1
    )
    row = jnp.sum(
        jnp.where(diagonal, jnp.broadcast_to(values, (count, width)), 0.0), axis=0, keepdims=True
    )
    row_ref[...] = jnp.broadcast_to(row, row_ref.shape)


def update_kernel(
    block_ref, rows_ref, curv_ref, band_ref, res_ref, iter_ref, delay_ref, res_delay_ref, iter_delay_ref,
    iter_out, iter_delay_out, res_out, res_delay_out, dir_out, dir_delay_out
):
    rows = rows_ref[...]
    count, width = rows.shape
    owned = band_ref.shape[0]
    half = 2 * owned
    sums = jnp.sum(rows, axis=0, keepdims=True)
    lane = lax.broadcasted_iota(jnp.int32, (1, width), 1)

    def scalar(x):
        return jnp.sum(x, axis=1, keepdims=True)

    pair = rows + pltpu.roll(rows, count - 1, 0)
    moves = pltpu.roll(rows, width - 16, 1)
    lefts = pltpu.roll(rows, width - 24, 1)
    curves = pair + damping_weight * moves
    valid = (lax.broadcasted_iota(jnp.int32, (count, width), 0) % 2 == 0) & (
        lax.broadcasted_iota(jnp.int32, (count, width), 1) < half
    )

    def delays(x):
        return scalar(jnp.sum(jnp.where(valid, x, 0.0), axis=0, keepdims=True))

    squares = scalar(jnp.where(lane == half, sums, 0.0)) + delays(lefts * lefts)
    cross = scalar(jnp.where(lane == half + 1, sums, 0.0)) + delays(lefts * curves)
    norm = scalar(jnp.where(lane == half + 2, sums, 0.0)) + delays(curves * curves)
    curvature = scalar(jnp.where(lane == half + 3, sums, 0.0)) + delays(moves * curves)
    alpha = squares / curvature
    fresh = squares + alpha * (alpha * norm - 2.0 * cross)
    ratio = fresh / squares

    band, curv = band_ref[...], curv_ref[...]
    alpha3 = alpha.reshape(1, 1, 1)
    ratio3 = ratio.reshape(1, 1, 1)
    iter_out[...] = iter_ref[...] + alpha3 * band
    new_res = res_ref[...] - alpha3 * curv
    res_out[...] = new_res
    dir_out[...] = new_res + ratio3 * band

    mine = lax.broadcasted_iota(jnp.int32, (count, width), 0) == 2 * block_ref[0]
    own = jnp.sum(jnp.where(mine, pair, 0.0), axis=0, keepdims=True)
    own = jnp.concatenate([own[:, 0:owned], own[:, owned:half]], axis=0)
    move = delay_ref[...]
    iter_delay_out[...] = iter_delay_ref[...] + alpha * move
    new_left = res_delay_ref[...] - alpha * (own + damping_weight * move)
    res_delay_out[...] = new_left
    dir_delay_out[...] = new_left + ratio * move


def body(
    gains,
    delays,
    model,
    antenna1,
    antenna2,
    dir_band,
    dir_delay,
    res_band,
    res_delay,
    iter_band,
    iter_delay,
):
    owned, _, width = gains.shape
    rows = model.shape[0]
    blocks = lax.axis_size("base")
    lines = lax.axis_size("z")
    cores = lax.axis_size("core")
    channels = width * lines * cores
    slots = 4 * owned
    factor = owned / (2.0 * rows)
    block = lax.axis_index("base").astype(jnp.int32)
    chan = (lax.axis_index("z") * cores + lax.axis_index("core")).astype(jnp.int32)
    block_one = block.reshape(1)
    place = jnp.stack([chan, lax.axis_index("z").astype(jnp.int32)])

    delays_t, dir_delay_t, res_delay_t, iter_delay_t = (
        jnp.transpose(x) for x in (delays, dir_delay, res_delay, iter_delay)
    )

    terms, turn = pl.pallas_call(
        lambda *refs: station_kernel(*refs, channels=channels),
        out_shape=(shape(16 * owned, width), shape(4 * owned, width)),
        in_specs=[smem()] + [vmem()] * 4,
        out_specs=(vmem(), vmem()),
        scratch_shapes=[pltpu.VMEM((16 * owned, width), f32)],
        compiler_params=params(4),
        name="station_terms",
    )(place, gains, dir_band, delays_t, dir_delay_t)

    def step(value, by):
        return lax.ppermute(value, "base", [(i, (i + by) % blocks) for i in range(blocks)])

    near_next, near_last, far = step(terms, -1), step(terms, 1), step(terms, blocks // 2)

    model_parts, gather, scatter = pl.pallas_call(
        lambda *refs: prepare_kernel(*refs, owned=owned, blocks=blocks),
        out_shape=(
            shape(8, rows, width),
            shape(2 * rows, 128, dtype=bf16),
            shape(slots, 2 * rows, dtype=bf16),
        ),
        in_specs=[smem()] + [vmem()] * 3,
        out_specs=(vmem(),) * 3,
        compiler_params=params(8),
        cost_estimate=pl.CostEstimate(flops=300000000, bytes_accessed=2000000, transcendentals=0),
        name="prepare",
    )(block_one, model.reshape(rows * 8, width), antenna1.reshape(1, rows), antenna2.reshape(1, rows))

    own, to_next, to_last, to_far = pl.pallas_call(
        lambda *refs: baseline_kernel(*refs, factor=factor),
        out_shape=(shape(8 * owned, width),) * 4,
        in_specs=[vmem()] * 7,
        out_specs=(vmem(),) * 4,
        scratch_shapes=[
            pltpu.VMEM((slots, 16 * width), f32),
            pltpu.VMEM((2 * rows, 16 * width), f32),
            pltpu.VMEM((2 * rows, 8 * width), f32),
        ],
        compiler_params=params(24),
        name="baselines",
    )(terms, near_next, near_last, far, model_parts, gather, scatter)

    from_last, from_next, from_far = step(to_next, 1), step(to_last, -1), step(to_far, blocks // 2)

    curv, row = pl.pallas_call(
        lambda *refs: curvature_kernel(*refs, channels=channels),
        out_shape=(shape(owned, 8, width), shape(lines, width)),
        in_specs=[smem()] + [vmem()] * 10,
        out_specs=(vmem(), vmem()),
        compiler_params=params(4),
        name="curvature",
    )(place, own, from_last, from_next, from_far, terms, turn, dir_band, res_band, dir_delay_t, res_delay_t)

    line = lax.all_to_all(row, "z", 0, 0, tiled=True)
    peers = blocks * cores
    line = jnp.broadcast_to(jnp.sum(line, axis=0, keepdims=True), (peers, width))
    everyone = lax.all_to_all(line, ("base", "core"), 0, 0, tiled=True)

    outs = pl.pallas_call(
        update_kernel,
        out_shape=(
            shape(owned, 8, width),
            shape(2, owned),
            shape(owned, 8, width),
            shape(2, owned),
            shape(owned, 8, width),
            shape(2, owned),
        ),
        in_specs=[smem()] + [vmem()] * 8,
        out_specs=(vmem(),) * 6,
        compiler_params=params(4),
        name="update",
    )(block_one, everyone, curv, dir_band, res_band, iter_band, dir_delay_t, res_delay_t, iter_delay_t)
    return (
        outs[0],
        jnp.transpose(outs[1]),
        outs[2],
        jnp.transpose(outs[3]),
        outs[4],
        jnp.transpose(outs[5]),
    )


def solution(mesh):
    cores = 2
    blocks, chans = mesh.shape["base"], mesh.shape["chan"]
    split = Mesh(mesh.devices.reshape(blocks, chans // cores, cores), ("base", "z", "core"))
    band = P("base", None, ("z", "core"))
    delay = P("base", None)
    one = P("base")
    return jax.shard_map(
        body,
        mesh=split,
        in_specs=(band, delay, band, one, one, band, delay, band, delay, band, delay),
        out_specs=(band, delay) * 3,
        check_vma=False,
    )
```

time: 595 us -> 79.1 us (0.13)
  blocking collectives: 296 us -> 33.7 us
  waiting for transfers between devices: 237 us -> 6.09 us
  starting transfers between devices: 0.04 us -> 27.8 us
  other arithmetic: 22 us -> 0.1 us
  between operations: 21.3 us -> 0.8 us
  local copies, waits for them, and re-layouts: 17.6 us -> 4.52 us
    reduce_scatter x1 -> x0, waiting for transfers between devices: 237 us -> none  [body(): lax.psum_scatter(station_grad.reshape(stations, 8, width), 'base', scatte...]
    psum x3 -> x0, blocking collectives: 220 us -> none  [the longest x1 95.2 us: body(): squares = lax.psum(squares_local, ('base', 'chan'))]
    all_gather x2 -> x0, blocking collectives: 75.6 us -> none  [the longest x1 39.9 us: body(): lax.all_gather(jones, 'base', axis=0, tiled=True)]
    all_to_all x0 -> x2, blocking collectives: none -> 33.7 us  [the longest x1 17.3 us: body(): everyone = lax.all_to_all(line, ('base', 'core'), 0, 0, tiled=True)]
    ppermute x0 -> x6, starting transfers between devices: none -> 27.8 us  [step(): lax.ppermute(value, 'base', [(i, (i + by) % blocks) for i in range(blocks)])]
    mul x5 -> x0, other arithmetic: 9.01 us -> none  [the longest x1 5.15 us: baseline_change(): multiplier_factor * (first[0] + second[0])]
    slice x19 -> x0, local copies, waits for them, and re-layouts: 6.97 us -> none  [the longest x12 4.88 us: matrix_product(): left[:, :, 0:1, :] * right[:, None, 0, :, :]]
    ppermute x0 -> x6, waiting for transfers between devices: none -> 6.09 us  [step(): lax.ppermute(value, 'base', [(i, (i + by) % blocks) for i in range(blocks)])]
  transfers between devices with their start and end apart: 1 -> 6, of which waited for: 1 -> 1; matrix products, arithmetic and copies ran while one was open for 0% -> 0% of each run, Pallas kernels for 0% -> 1%
where the time goes in v1:
time: 79.1 us; the launch traced here: 78.5 us
  blocking collectives  33.7 us (43%)
  starting transfers between devices  27.8 us (35%)
  waiting for transfers between devices  6.09 us (8%)
  Pallas kernels  5.52 us (7%)
  local copies, waits for them, and re-layouts  4.52 us (6%)
  between operations  0.8 us (1%)
    ppermute x6, starting transfers between devices, step(): lax.ppermute(value, 'base', [(i, (i + by) % blocks) for i in range(blocks)])  27.8 us
    all_to_all x1, blocking collectives, body(): everyone = lax.all_to_all(line, ('base', 'core'), 0, 0, tiled=True)  17.3 us
    all_to_all x1, blocking collectives, body(): line = lax.all_to_all(row, 'z', 0, 0, tiled=True)  16.4 us
    ppermute x6, waiting for transfers between devices, step(): lax.ppermute(value, 'base', [(i, (i + by) % blocks) for i in range(blocks)])  6.09 us
    unnamed x22, local copies, waits for them, and re-layouts  4.5 us
    pallas_call x1, Pallas kernels, body(): pl.pallas_call(lambda *refs: baseline_kernel(*refs, factor=factor), out_s...  2.77 us
  transfers between devices with their start and end apart: 6, of which 1 were waited for; matrix products, arithmetic and copies ran while one was open for 0% of the time, Pallas kernels for 1%

profile of v1, /device:TPU:1, one launch (start us, length us, event | category | flops | bytes accessed | tf_op | source)
XLA Modules:
  0.0 78.5 jit_solution(8708149733858181912)
XLA Ops:
  0.6 0.0 copy-start
  0.6 0.1 pad_add_fusion.refs_0_
  0.7 0.0 copy-start.7
  0.7 0.0 copy-start.4
  0.7 0.6 copy-done
  1.4 0.1 copy-done.7
  1.4 0.0 copy-done.4
  1.4 0.0 copy-start.3
  1.4 0.7 copy-done.3
  2.1 0.8 %station_terms.1 = (f32[64,128]{1,0:T(8,128)S(1)}, f32[16,128]{1,0:T(8,128)S(1)}) custom-call(s32[2]{0:T(128)S(1)} %pad_add_fusion.refs_0_, f32[4,8,128]{2,1,0:T(8,128)S(1)} %copy-done.3, f32[4,8,128]{2,1,0:T(8,128)S(1)} %copy-done, f32[2,4]{1,0:T(2,128)S(1)} %bitcast.25, f32[2,4]{1,0:T(2,128)S(1)} %bitcast.18), custom_call_target="tpu_custom_call" | custom-call | tf_op jit(solution)/shard_map/station_terms/pallas_call | solution.py:352
  2.9 8.3 %collective-permute-start.2 = (f32[64,128]{1,0:T(8,128)S(1)}, f32[64,128]{1,0:T(8,128)S(1)}, u32[]{:S(2)}, u32[]{:S(2)}) collective-permute-start(f32[64,128]{1,0:T(8,128)S(1)} %get-tuple-element.23.refs_0_.refs_5_), channel_id=1, source_target_pairs={{0,256},{16,272},{32,288},{48,304},{64,320},{80,336},{96,352},{112... | collective-permute-start | bytes 98312 | tf_op jit(solution)/shard_map/ppermute | solution.py:363
  11.2 3.1 %collective-permute-start.1 = (f32[64,128]{1,0:T(8,128)S(1)}, f32[64,128]{1,0:T(8,128)S(1)}, u32[]{:S(2)}, u32[]{:S(2)}) collective-permute-start(f32[64,128]{1,0:T(8,128)S(1)} %get-tuple-element.23.refs_0_.refs_5_), channel_id=1, source_target_pairs={{0,16},{16,32},{32,48},{48,64},{64,80},{80,96},{96,112},{112,128},... | collective-permute-start | bytes 98312 | tf_op jit(solution)/shard_map/ppermute | solution.py:363
  14.3 5.5 %collective-permute-start = (f32[64,128]{1,0:T(8,128)S(1)}, f32[64,128]{1,0:T(8,128)S(1)}, u32[]{:S(2)}, u32[]{:S(2)}) collective-permute-start(f32[64,128]{1,0:T(8,128)S(1)} %get-tuple-element.23.refs_0_.refs_5_), channel_id=1, source_target_pairs={{0,496},{16,0},{32,16},{48,32},{64,48},{80,64},{96,80},{112,96},{1... | collective-permute-start | bytes 98312 | tf_op jit(solution)/shard_map/ppermute | solution.py:363
  19.8 0.0 copy-start.10
  19.9 0.0 copy-start.9
  19.9 0.7 copy-done.10
  20.5 0.0 copy-done.9
  20.5 0.0 copy-start.8
  20.5 1.0 %copy-done.8 = bf16[256,8,128]{2,1,0:T(8,128)(2,1)S(1)} copy-done((bf16[256,8,128]{2,1,0:T(8,128)(2,1)S(1)}, bf16[256,8,128]{2,1,0:T(8,128)(2,1)}, u32[]{:S(2)}) %copy-start.8) | copy-done | bytes 524312
  21.6 0.4 prepare.1
  22.0 0.0 collective-permute-done.2.refs_3_
  22.0 0.0 collective-permute-done.1.refs_2_
  22.0 0.0 collective-permute-done.refs_1_
  22.0 0.0 copy-start.1
  22.1 2.8 %baselines.1 = (f32[32,128]{1,0:T(8,128)S(1)}, f32[32,128]{1,0:T(8,128)S(1)}, f32[32,128]{1,0:T(8,128)S(1)}, f32[32,128]{1,0:T(8,128)S(1)}) custom-call(f32[64,128]{1,0:T(8,128)S(1)} %get-tuple-element.23.refs_0_.refs_5_, f32[64,128]{1,0:T(8,128)S(1)} %collective-permute-done.refs_1_, f32[64,128]{1,0:T(8,128)S(1)} %collective-permute-done.1.refs_2_, ...), custom_call_target="tpu_custom_call" | custom-call | tf_op jit(solution)/shard_map/baselines/pallas_call | solution.py:381
  24.8 1.9 %collective-permute-start.3 = (f32[32,128]{1,0:T(8,128)S(1)}, f32[32,128]{1,0:T(8,128)S(1)}, u32[]{:S(2)}, u32[]{:S(2)}) collective-permute-start(f32[32,128]{1,0:T(8,128)S(1)} %get-tuple-element.28), channel_id=1, source_target_pairs={{0,16},{16,32},{32,48},{48,64},{64,80},{80,96},{96,112},{112,128},... | collective-permute-start | bytes 49160 | tf_op jit(solution)/shard_map/ppermute | solution.py:363
  26.8 6.7 %collective-permute-start.4 = (f32[32,128]{1,0:T(8,128)S(1)}, f32[32,128]{1,0:T(8,128)S(1)}, u32[]{:S(2)}, u32[]{:S(2)}) collective-permute-start(f32[32,128]{1,0:T(8,128)S(1)} %get-tuple-element.29), channel_id=1, source_target_pairs={{0,496},{16,0},{32,16},{48,32},{64,48},{80,64},{96,80},{112,96},{1... | collective-permute-start | bytes 49160 | tf_op jit(solution)/shard_map/ppermute | solution.py:363
  33.5 2.3 %collective-permute-start.5 = (f32[32,128]{1,0:T(8,128)S(1)}, f32[32,128]{1,0:T(8,128)S(1)}, u32[]{:S(2)}, u32[]{:S(2)}) collective-permute-start(f32[32,128]{1,0:T(8,128)S(1)} %get-tuple-element.30), channel_id=1, source_target_pairs={{0,256},{16,272},{32,288},{48,304},{64,320},{80,336},{96,352},{112... | collective-permute-start | bytes 49160 | tf_op jit(solution)/shard_map/ppermute | solution.py:363
  35.8 0.0 collective-permute-done.3.refs_2_
  35.8 0.0 collective-permute-done.4.refs_3_
  35.8 6.1 %collective-permute-done.5.refs_4_ = f32[32,128]{1,0:T(8,128)S(1)} collective-permute-done((f32[32,128]{1,0:T(8,128)S(1)}, f32[32,128]{1,0:T(8,128)S(1)}, u32[]{:S(2)}, u32[]{:S(2)}) %collective-permute-start.5) | collective-permute-done | bytes 16416 | tf_op jit(solution)/shard_map/ppermute | solution.py:363
  41.9 0.0 copy-start.5
  41.9 0.0 copy-done.1
  41.9 0.7 copy-done.5
  42.6 0.7 curvature.1
  43.3 16.4 %all_to_all.17 = f32[8,1,128]{2,1,0:T(1,128)S(1)} all-to-all(f32[8,1,128]{2,1,0:T(1,128)S(1)} %bitcast.23), channel_id=1, replica_groups=mesh['base'=32,'z'=8,'core'=2] {'z'}, dimensions={0} | all-to-all | bytes 8192 | tf_op jit(solution)/shard_map/all_to_all | solution.py:406
  59.7 0.0 copy-start.2
  59.7 17.3 %all_to_all.18 = f32[64,1,128]{2,1,0:T(1,128)S(1)} all-to-all(f32[64,1,128]{2,1,0:T(1,128)S(1)} %broadcast_in_dim.2), channel_id=1, replica_groups=mesh['base'=32,'z'=8,'core'=2] {'base','core'}, dimensions={0} | all-to-all | bytes 65536 | tf_op jit(solution)/shard_map/all_to_all | solution.py:409
  77.1 0.0 copy-start.6
  77.1 0.0 copy-done.2
  77.1 0.7 copy-done.6
  77.7 0.8 %update.1 = (f32[4,8,128]{2,1,0:T(8,128)}, f32[2,4]{1,0:T(2,128)}, f32[4,8,128]{2,1,0:T(8,128)}, f32[2,4]{1,0:T(2,128)}, f32[4,8,128]{2,1,0:T(8,128)}, /*index=5*/f32[2,4]{1,0:T(2,128)}) custom-call(s32[1]{0:T(128)} %bitcast.refs_0_.block_ref, f32[64,128]{1,0:T(8,128)S(1)} %bitcast.17, f32[4,8,128]{2,1,0:T(8,128)S(1)} %get-tuple-element.33.curv_ref, ...), custom_call_target="tpu_custom_call" | custom-call | tf_op jit(solution)/shard_map/update/pallas_call | solution.py:411
  (2 shorter events, 0.0 us)
Async XLA Ops:
  0.6 0.7 copy-start
  0.7 0.7 copy-start.7
  0.7 0.7 copy-start.4
  1.4 0.7 copy-start.3
  2.9 19.1 %collective-permute-start.2 = (f32[64,128]{1,0:T(8,128)S(1)}, f32[64,128]{1,0:T(8,128)S(1)}, u32[]{:S(2)}, u32[]{:S(2)}) collective-permute-start(f32[64,128]{1,0:T(8,128)S(1)} %get-tuple-element.23.refs_0_.refs_5_), channel_id=1, source_target_pairs={{0,256},{16,272},{32,288},{48,304},{64,320},{80,336},{96,352},{112... | collective-permute-start | bytes 98312 | tf_op jit(solution)/shard_map/ppermute | solution.py:363
  11.2 10.8 %collective-permute-start.1 = (f32[64,128]{1,0:T(8,128)S(1)}, f32[64,128]{1,0:T(8,128)S(1)}, u32[]{:S(2)}, u32[]{:S(2)}) collective-permute-start(f32[64,128]{1,0:T(8,128)S(1)} %get-tuple-element.23.refs_0_.refs_5_), channel_id=1, source_target_pairs={{0,16},{16,32},{32,48},{48,64},{64,80},{80,96},{96,112},{112,128},... | collective-permute-start | bytes 98312 | tf_op jit(solution)/shard_map/ppermute | solution.py:363
  14.3 7.7 %collective-permute-start = (f32[64,128]{1,0:T(8,128)S(1)}, f32[64,128]{1,0:T(8,128)S(1)}, u32[]{:S(2)}, u32[]{:S(2)}) collective-permute-start(f32[64,128]{1,0:T(8,128)S(1)} %get-tuple-element.23.refs_0_.refs_5_), channel_id=1, source_target_pairs={{0,496},{16,0},{32,16},{48,32},{64,48},{80,64},{96,80},{112,96},{1... | collective-permute-start | bytes 98312 | tf_op jit(solution)/shard_map/ppermute | solution.py:363
  19.8 0.7 copy-start.10
  19.9 0.7 copy-start.9
  20.5 1.0 %copy-start.8 = (bf16[256,8,128]{2,1,0:T(8,128)(2,1)S(1)}, bf16[256,8,128]{2,1,0:T(8,128)(2,1)}, u32[]{:S(2)}) copy-start(bf16[256,8,128]{2,1,0:T(8,128)(2,1)} %param.13) | copy-start | bytes 1572868
  22.0 19.9 %copy-start.1 = (f32[4,8,128]{2,1,0:T(8,128)S(1)}, f32[4,8,128]{2,1,0:T(8,128)}, u32[]{:S(2)}) copy-start(f32[4,8,128]{2,1,0:T(8,128)} %res_ref.1) | copy-start | bytes 49156
  24.8 11.0 %collective-permute-start.3 = (f32[32,128]{1,0:T(8,128)S(1)}, f32[32,128]{1,0:T(8,128)S(1)}, u32[]{:S(2)}, u32[]{:S(2)}) collective-permute-start(f32[32,128]{1,0:T(8,128)S(1)} %get-tuple-element.28), channel_id=1, source_target_pairs={{0,16},{16,32},{32,48},{48,64},{64,80},{80,96},{96,112},{112,128},... | collective-permute-start | bytes 49160 | tf_op jit(solution)/shard_map/ppermute | solution.py:363
  26.8 9.1 %collective-permute-start.4 = (f32[32,128]{1,0:T(8,128)S(1)}, f32[32,128]{1,0:T(8,128)S(1)}, u32[]{:S(2)}, u32[]{:S(2)}) collective-permute-start(f32[32,128]{1,0:T(8,128)S(1)} %get-tuple-element.29), channel_id=1, source_target_pairs={{0,496},{16,0},{32,16},{48,32},{64,48},{80,64},{96,80},{112,96},{1... | collective-permute-start | bytes 49160 | tf_op jit(solution)/shard_map/ppermute | solution.py:363
  33.5 8.4 %collective-permute-start.5 = (f32[32,128]{1,0:T(8,128)S(1)}, f32[32,128]{1,0:T(8,128)S(1)}, u32[]{:S(2)}, u32[]{:S(2)}) collective-permute-start(f32[32,128]{1,0:T(8,128)S(1)} %get-tuple-element.30), channel_id=1, source_target_pairs={{0,256},{16,272},{32,288},{48,304},{64,320},{80,336},{96,352},{112... | collective-permute-start | bytes 49160 | tf_op jit(solution)/shard_map/ppermute | solution.py:363
  41.9 0.7 copy-start.5
  59.7 17.3 %copy-start.2 = (f32[4,8,128]{2,1,0:T(8,128)S(1)}, f32[4,8,128]{2,1,0:T(8,128)}, u32[]{:S(2)}) copy-start(f32[4,8,128]{2,1,0:T(8,128)} %iter_ref.1) | copy-start | bytes 49156
  77.1 0.7 copy-start.6

commit v2 on v1

--- a/solution.py
+++ b/solution.py
@@ -19,16 +19,20 @@
     return pl.BlockSpec(memory_space=pltpu.VMEM)
 
 
-def smem():
-    return pl.BlockSpec(memory_space=pltpu.SMEM)
+def hbm():
+    return pl.BlockSpec(memory_space=pltpu.HBM)
 
 
 def params(mib):
-    return pltpu.CompilerParams(vmem_limit_bytes=mib * 1024 * 1024)
+    return pltpu.CompilerParams(vmem_limit_bytes=int(mib * 1024 * 1024))
 
 
 def shape(*dims, dtype=f32):
     return jax.ShapeDtypeStruct(dims, dtype)
+
+
+def chan_index():
+    return lax.axis_index("z") * lax.axis_size("core") + lax.axis_index("core")
 
 
 def frequencies(chan, width, channels):
@@ -52,19 +56,58 @@
     return jnp.concatenate(parts, axis=0)
 
 
+def pick_stations(ids, gather_ref, scatter_ref, *, owned, blocks):
+    rows = ids.shape[1]
+    slots = 4 * owned
+    slot = lax.broadcasted_iota(jnp.int32, (slots, 2 * rows), 0)
+    kind = slot // owned
+    block = lax.axis_index("base")
+    turn_up = 1 - 2 * (block % 2)
+    offset = jnp.where(kind == 0, 0, jnp.where(kind == 1, turn_up, jnp.where(kind == 2, -turn_up, blocks // 2)))
+    station = ((block + offset + blocks) % blocks) * owned + slot % owned
+    both = jnp.concatenate([ids[0:1, :], ids[1:2, :]], axis=1)
+    pick = jnp.where(station == both, 1.0, 0.0)
+    filled = jnp.concatenate([pick] * 3 + [jnp.zeros((128 - 3 * slots, 2 * rows), f32)], axis=0)
+    scatter_ref[...] = pick.astype(bf16)
+    gather_ref[...] = jnp.transpose(filled).astype(bf16)
+
+
 def station_kernel(
-    chan_ref, gains_ref, band_ref, delays_ref, move_ref, terms_ref, turn_ref, packed, *, channels
+    gains_hbm, band_hbm, delays_hbm, move_hbm, left_hbm, iter_hbm, first_hbm, second_hbm, model_hbm,
+    terms_ref, turn_ref, small_ref, gather_ref, scatter_ref, model_ref,
+    gains_ref, band_ref, delays_ref, ids, packed, sems, *, channels, blocks
 ):
     owned, _, width = gains_ref.shape
     half = 2 * owned
+    pairs = [
+        (first_hbm, ids.at[0:1]),
+        (second_hbm, ids.at[1:2]),
+        (delays_hbm, delays_ref),
+        (move_hbm, small_ref.at[0]),
+        (gains_hbm, gains_ref),
+        (band_hbm, band_ref),
+        (model_hbm, model_ref),
+        (left_hbm, small_ref.at[1]),
+        (iter_hbm, small_ref.at[2]),
+    ]
+    copies = [pltpu.make_async_copy(a, b, sems.at[k]) for k, (a, b) in enumerate(pairs)]
+    for copy in copies:
+        copy.start()
+    copies[0].wait()
+    copies[1].wait()
+    pick_stations(ids, gather_ref, scatter_ref, owned=owned, blocks=blocks)
+    copies[2].wait()
+    copies[3].wait()
     delay_scale = channels ** (-0.5)
-    freq = frequencies(chan_ref[0], width, channels)
+    freq = frequencies(chan_index(), width, channels)
     phase = full_turn * column(delays_ref) * freq
-    rate = full_turn * delay_scale * column(move_ref) * freq
+    rate = full_turn * delay_scale * column(small_ref.at[0]) * freq
     cosine = jnp.cos(phase)
     sine = jnp.sin(phase)
     turn_ref[0:half, :] = cosine
     turn_ref[half : 2 * half, :] = sine
+    copies[4].wait()
+    copies[5].wait()
     for j in range(8):
         packed[j * owned : (j + 1) * owned, :] = gains_ref[:, j, :]
         packed[(8 + j) * owned : (9 + j) * owned, :] = band_ref[:, j, :]
@@ -83,34 +126,8 @@
         terms_ref[move_im, :] = (
             cosine * packed[move_im, :] + sine * packed[move_re, :] + rate * jones_re
         )
-
-
-def prepare_kernel(block_ref, model_ref, first_ref, second_ref, model_out, gather_out, scatter_out, *, owned, blocks):
-    rows = first_ref.shape[1]
-    width = model_ref.shape[1]
-    group = 32
-    block = block_ref[0]
-    size = 8 * group
-    out_row = lax.broadcasted_iota(jnp.int32, (size, size), 0)
-    in_row = lax.broadcasted_iota(jnp.int32, (size, size), 1)
-    wanted = (out_row % group) * 8 + out_row // group
-    shuffle = jnp.where(in_row == wanted, 1.0, 0.0).astype(bf16)
-    for g in range(rows // group):
-        part = jnp.dot(
-            shuffle, model_ref[g * size : (g + 1) * size, :], preferred_element_type=f32
-        )
-        for j in range(8):
-            model_out[j, g * group : (g + 1) * group, :] = part[j * group : (j + 1) * group, :]
-    slots = 4 * owned
-    slot = lax.broadcasted_iota(jnp.int32, (slots, 2 * rows), 0)
-    kind = slot // owned
-    offset = jnp.where(kind == 0, 0, jnp.where(kind == 1, 1, jnp.where(kind == 2, blocks - 1, blocks // 2)))
-    station = ((block + offset) % blocks) * owned + slot % owned
-    both = jnp.concatenate([first_ref[...], second_ref[...]], axis=1)
-    pick = jnp.where(station == both, 1.0, 0.0)
-    scatter_out[...] = pick.astype(bf16)
-    filled = jnp.concatenate([pick] * 3 + [jnp.zeros((128 - 3 * slots, 2 * rows), f32)], axis=0)
-    gather_out[...] = jnp.transpose(filled).astype(bf16)
+    for copy in copies[6:]:
+        copy.wait()
 
 
 def times(a, b):
@@ -165,13 +182,17 @@
 
 
 def baseline_kernel(
-    own_ref, next_ref, last_ref, far_ref, model_ref, gather_ref, scatter_ref,
-    own_out, next_out, last_out, far_out, table, picked, grads, *, factor
+    own_ref, even_ref, odd_ref, far_ref, model_ref, gather_ref, scatter_ref,
+    own_out, even_out, odd_out, far_out, table, picked, grads, model_parts, *, factor
 ):
-    _, rows, width = model_ref.shape
+    _, rows, width = model_parts.shape
     slots = table.shape[0]
     owned = slots // 4
-    for k, ref in enumerate((own_ref, next_ref, last_ref, far_ref)):
+    group = 32
+    size = 8 * group
+    pick, scatter = gather_ref[...], scatter_ref[...]
+    partner = odd_ref.at[lax.axis_index("base") % 2]
+    for k, ref in enumerate((own_ref, even_ref, partner, far_ref)):
         for j in range(16):
             table[k * owned : (k + 1) * owned, j * width : (j + 1) * width] = ref[
                 j * owned : (j + 1) * owned, :
@@ -184,16 +205,26 @@
     split = jnp.concatenate(
         [high, middle, low, jnp.zeros((128 - 3 * slots, exact.shape[1]), bf16)], axis=0
     )
-    pick = gather_ref[...]
     step = 2 * width
     for n in range(0, 16 * width, step):
         picked[:, n : n + step] = jnp.dot(pick, split[:, n : n + step], preferred_element_type=f32)
+
+    out_row = lax.broadcasted_iota(jnp.int32, (size, size), 0)
+    in_row = lax.broadcasted_iota(jnp.int32, (size, size), 1)
+    wanted = (out_row % group) * 8 + out_row // group
+    shuffle = jnp.where(in_row == wanted, 1.0, 0.0).astype(bf16)
+    for g in range(rows // group):
+        part = jnp.dot(
+            shuffle, model_ref[g * size : (g + 1) * size, :], preferred_element_type=f32
+        )
+        for j in range(8):
+            model_parts[j, g * group : (g + 1) * group, :] = part[j * group : (j + 1) * group, :]
 
     def chunk(i, carry):
         at = pl.ds(pl.multiple_of(i * 8, 8), 8)
         at_q = pl.ds(pl.multiple_of(rows + i * 8, 8), 8)
         cols = [slice(j * width, (j + 1) * width) for j in range(16)]
-        model = [model_ref[j, at, :] for j in range(8)]
+        model = [model_parts[j, at, :] for j in range(8)]
         right = times_adjoint(model, [picked[at_q, c] for c in cols[:8]])
         left = times([picked[at, c] for c in cols[:8]], model)
         one = times([picked[at, c] for c in cols[8:]], right)
@@ -211,11 +242,11 @@
         value = grads[:, n : n + step]
         high = value.astype(bf16)
         low = (value - high.astype(f32)).astype(bf16)
-        total = jnp.dot(scatter_ref[...], high, preferred_element_type=f32) + jnp.dot(
-            scatter_ref[...], low, preferred_element_type=f32
+        total = jnp.dot(scatter, high, preferred_element_type=f32) + jnp.dot(
+            scatter, low, preferred_element_type=f32
         )
         table[:, n : n + step] = factor * total
-    for k, ref in enumerate((own_out, next_out, last_out, far_out)):
+    for k, ref in enumerate((own_out, even_out, odd_out, far_out)):
         for j in range(8):
             ref[j * owned : (j + 1) * owned, :] = table[
                 k * owned : (k + 1) * owned, j * width : (j + 1) * width
@@ -223,16 +254,16 @@
 
 
 def curvature_kernel(
-    place_ref, own_ref, a_ref, b_ref, c_ref, terms_ref, turn_ref, band_ref, res_ref, delay_ref, res_delay_ref,
+    own_ref, even_ref, odd_ref, far_ref, terms_ref, turn_ref, small_ref, band_ref, res_ref,
     curv_ref, row_ref, *, channels
 ):
     owned, _, width = band_ref.shape
     half = 2 * owned
     delay_scale = channels ** (-0.5)
-    freq = frequencies(place_ref[0], width, channels)
+    freq = frequencies(chan_index(), width, channels)
     cosine = turn_ref[0:half, :]
     sine = turn_ref[half : 2 * half, :]
-    total = own_ref[...] + a_ref[...] + b_ref[...] + c_ref[...]
+    total = own_ref[...] + even_ref[...] + odd_ref[lax.axis_index("base") % 2] + far_ref[...]
     moved = jnp.zeros((half, width), f32)
     for r in range(2):
         re = slice(r * half, (r + 1) * half)
@@ -252,10 +283,10 @@
         jnp.sum(jnp.sum(jnp.sum(x, axis=0), axis=0, keepdims=True), axis=1, keepdims=True)
         for x in (res * res, res * curv, curv * curv, band * curv)
     ]
-    here = jnp.where(place_ref[1] == 0, 1.0, 0.0)
+    here = jnp.where(lax.axis_index("z") == 0, 1.0, 0.0)
     values = jnp.concatenate(
         [moved] + scalars + [jnp.zeros((4, 1), f32)]
-        + [here * column(delay_ref), here * column(res_delay_ref)],
+        + [here * column(small_ref.at[0]), here * column(small_ref.at[1])],
         axis=0,
     )
     count = values.shape[0]
@@ -269,7 +300,7 @@
 
 
 def update_kernel(
-    block_ref, rows_ref, curv_ref, band_ref, res_ref, iter_ref, delay_ref, res_delay_ref, iter_delay_ref,
+    rows_ref, curv_ref, small_ref, band_ref, res_ref, iter_ref,
     iter_out, iter_delay_out, res_out, res_delay_out, dir_out, dir_delay_out
 ):
     rows = rows_ref[...]
@@ -309,12 +340,12 @@
     res_out[...] = new_res
     dir_out[...] = new_res + ratio3 * band
 
-    mine = lax.broadcasted_iota(jnp.int32, (count, width), 0) == 2 * block_ref[0]
+    mine = lax.broadcasted_iota(jnp.int32, (count, width), 0) == 2 * lax.axis_index("base")
     own = jnp.sum(jnp.where(mine, pair, 0.0), axis=0, keepdims=True)
     own = jnp.concatenate([own[:, 0:owned], own[:, owned:half]], axis=0)
-    move = delay_ref[...]
-    iter_delay_out[...] = iter_delay_ref[...] + alpha * move
-    new_left = res_delay_ref[...] - alpha * (own + damping_weight * move)
+    move = small_ref[0]
+    iter_delay_out[...] = small_ref[2] + alpha * move
+    new_left = small_ref[1] - alpha * (own + damping_weight * move)
     res_delay_out[...] = new_left
     dir_delay_out[...] = new_left + ratio * move
 
@@ -340,45 +371,53 @@
     channels = width * lines * cores
     slots = 4 * owned
     factor = owned / (2.0 * rows)
-    block = lax.axis_index("base").astype(jnp.int32)
-    chan = (lax.axis_index("z") * cores + lax.axis_index("core")).astype(jnp.int32)
-    block_one = block.reshape(1)
-    place = jnp.stack([chan, lax.axis_index("z").astype(jnp.int32)])
-
     delays_t, dir_delay_t, res_delay_t, iter_delay_t = (
         jnp.transpose(x) for x in (delays, dir_delay, res_delay, iter_delay)
     )
 
-    terms, turn = pl.pallas_call(
-        lambda *refs: station_kernel(*refs, channels=channels),
-        out_shape=(shape(16 * owned, width), shape(4 * owned, width)),
-        in_specs=[smem()] + [vmem()] * 4,
-        out_specs=(vmem(), vmem()),
-        scratch_shapes=[pltpu.VMEM((16 * owned, width), f32)],
+    terms, turn, small, gather, scatter, model_local = pl.pallas_call(
+        lambda *refs: station_kernel(*refs, channels=channels, blocks=blocks),
+        out_shape=(
+            shape(16 * owned, width),
+            shape(4 * owned, width),
+            shape(3, 2, owned),
+            shape(2 * rows, 128, dtype=bf16),
+            shape(slots, 2 * rows, dtype=bf16),
+            shape(8 * rows, width, dtype=bf16),
+        ),
+        in_specs=[hbm()] * 9,
+        out_specs=(vmem(),) * 6,
+        scratch_shapes=[
+            pltpu.VMEM((owned, 8, width), f32),
+            pltpu.VMEM((owned, 8, width), f32),
+            pltpu.VMEM((2, owned), f32),
+            pltpu.VMEM((2, rows), jnp.int32),
+            pltpu.VMEM((16 * owned, width), f32),
+            pltpu.SemaphoreType.DMA((9,)),
+        ],
         compiler_params=params(4),
         name="station_terms",
-    )(place, gains, dir_band, delays_t, dir_delay_t)
-
-    def step(value, by):
-        return lax.ppermute(value, "base", [(i, (i + by) % blocks) for i in range(blocks)])
-
-    near_next, near_last, far = step(terms, -1), step(terms, 1), step(terms, blocks // 2)
-
-    model_parts, gather, scatter = pl.pallas_call(
-        lambda *refs: prepare_kernel(*refs, owned=owned, blocks=blocks),
-        out_shape=(
-            shape(8, rows, width),
-            shape(2 * rows, 128, dtype=bf16),
-            shape(slots, 2 * rows, dtype=bf16),
-        ),
-        in_specs=[smem()] + [vmem()] * 3,
-        out_specs=(vmem(),) * 3,
-        compiler_params=params(8),
-        cost_estimate=pl.CostEstimate(flops=300000000, bytes_accessed=2000000, transcendentals=0),
-        name="prepare",
-    )(block_one, model.reshape(rows * 8, width), antenna1.reshape(1, rows), antenna2.reshape(1, rows))
-
-    own, to_next, to_last, to_far = pl.pallas_call(
+    )(
+        *(
+            pltpu.with_memory_space_constraint(x, pltpu.HBM)
+            for x in (
+                gains, dir_band, delays_t, dir_delay_t, res_delay_t, iter_delay_t,
+                antenna1.reshape(1, rows), antenna2.reshape(1, rows), model.reshape(rows * 8, width),
+            )
+        )
+    )
+
+    far_pairs = [(i, (i + blocks // 2) % blocks) for i in range(blocks)]
+    even_pairs = [(i, i ^ 1) for i in range(blocks)]
+    odd_groups = [[i, (i + 1) % blocks] for i in range(1, blocks, 2)]
+
+    def exchange(to_even, to_odd, to_far):
+        far = lax.ppermute(to_far, "base", far_pairs)
+        even = lax.ppermute(to_even, "base", even_pairs)
+        odd = lax.all_gather(to_odd, "base", axis_index_groups=odd_groups)
+        return even, odd, far
+
+    own, to_even, to_odd, to_far = pl.pallas_call(
         lambda *refs: baseline_kernel(*refs, factor=factor),
         out_shape=(shape(8 * owned, width),) * 4,
         in_specs=[vmem()] * 7,
@@ -387,21 +426,23 @@
             pltpu.VMEM((slots, 16 * width), f32),
             pltpu.VMEM((2 * rows, 16 * width), f32),
             pltpu.VMEM((2 * rows, 8 * width), f32),
+            pltpu.VMEM((8, rows, width), f32),
         ],
         compiler_params=params(24),
         name="baselines",
-    )(terms, near_next, near_last, far, model_parts, gather, scatter)
-
-    from_last, from_next, from_far = step(to_next, 1), step(to_last, -1), step(to_far, blocks // 2)
+    )(
+        terms, *exchange(terms, terms, terms),
+        model_local, gather, scatter,
+    )
 
     curv, row = pl.pallas_call(
         lambda *refs: curvature_kernel(*refs, channels=channels),
         out_shape=(shape(owned, 8, width), shape(lines, width)),
-        in_specs=[smem()] + [vmem()] * 10,
+        in_specs=[vmem()] * 9,
         out_specs=(vmem(), vmem()),
         compiler_params=params(4),
         name="curvature",
-    )(place, own, from_last, from_next, from_far, terms, turn, dir_band, res_band, dir_delay_t, res_delay_t)
+    )(own, *exchange(to_even, to_odd, to_far), terms, turn, small, dir_band, res_band)
 
     line = lax.all_to_all(row, "z", 0, 0, tiled=True)
     peers = blocks * cores
@@ -418,11 +459,11 @@
             shape(owned, 8, width),
             shape(2, owned),
         ),
-        in_specs=[smem()] + [vmem()] * 8,
+        in_specs=[vmem()] * 6,
         out_specs=(vmem(),) * 6,
         compiler_params=params(4),
         name="update",
-    )(block_one, everyone, curv, dir_band, res_band, iter_band, dir_delay_t, res_delay_t, iter_delay_t)
+    )(everyone, curv, small, dir_band, res_band, iter_band)
     return (
         outs[0],
         jnp.transpose(outs[1]),

time: 79.1 us -> 73.3 us (0.927)
  blocking collectives: 33.7 us -> 51.6 us
  starting transfers between devices: 27.8 us -> 15.3 us
  waiting for transfers between devices: 6.09 us -> 0.01 us
  local copies, waits for them, and re-layouts: 4.52 us -> 0.04 us
    all_gather x0 -> x2, blocking collectives: none -> 13.4 us  [exchange(): odd = lax.all_gather(to_odd, 'base', axis_index_groups=odd_groups)]
    ppermute x6 -> x4, starting transfers between devices: 27.8 us -> 15.3 us  [the longest x2 10.2 us: exchange(): far = lax.ppermute(to_far, 'base', far_pairs)]
    ppermute x6 -> x4, waiting for transfers between devices: 6.09 us -> 0.01 us  [the longest x2 0.01 us: exchange(): even = lax.ppermute(to_even, 'base', even_pairs)]
    all_to_all x1, blocking collectives: 17.3 us -> 21.9 us  [body(): everyone = lax.all_to_all(line, ('base', 'core'), 0, 0, tiled=True)]
    unnamed x22 -> x6, local copies, waits for them, and re-layouts: 4.5 us -> 0.02 us
  transfers between devices with their start and end apart: 6 -> 4, of which waited for: 1 -> 0; matrix products, arithmetic and copies ran while one was open for 0% -> 0% of each run, Pallas kernels for 1% -> 0%
where the time goes in v2:
time: 73.3 us; the launch traced here: 72.9 us
  blocking collectives  51.6 us (70%)
  starting transfers between devices  15.3 us (21%)
  Pallas kernels  5.28 us (7%)
    all_to_all x1, blocking collectives, body(): everyone = lax.all_to_all(line, ('base', 'core'), 0, 0, tiled=True)  21.9 us
    all_to_all x1, blocking collectives, body(): line = lax.all_to_all(row, 'z', 0, 0, tiled=True)  16.4 us
    all_gather x2, blocking collectives, exchange(): odd = lax.all_gather(to_odd, 'base', axis_index_groups=odd_groups)  13.4 us
    ppermute x2, starting transfers between devices, exchange(): far = lax.ppermute(to_far, 'base', far_pairs)  10.2 us
    ppermute x2, starting transfers between devices, exchange(): even = lax.ppermute(to_even, 'base', even_pairs)  5.04 us
    pallas_call x1, Pallas kernels, body(): pl.pallas_call(lambda *refs: baseline_kernel(*refs, factor=factor), out_s...  3.05 us
  transfers between devices with their start and end apart: 4, of which 0 were waited for; matrix products, arithmetic and copies ran while one was open for 0% of the time, Pallas kernels for 0%

profile of v2, /device:TPU:1, one launch (start us, length us, event | category | flops | bytes accessed | tf_op | source)
XLA Modules:
  0.0 72.9 jit_solution(16281839331826166580)
XLA Ops:
  0.6 1.2 %station_terms.1 = (f32[64,128]{1,0:T(8,128)S(1)}, f32[16,128]{1,0:T(8,128)S(1)}, f32[3,2,4]{2,1,0:T(2,128)S(1)}, bf16[512,128]{1,0:T(8,128)(2,1)S(1)}, bf16[16,...) custom-call(f32[4,8,128]{2,1,0:T(8,128)} %refs_0_.1, f32[4,8,128]{2,1,0:T(8,128)} %band_ref.1, f32[2,4]{1,0:T(2,128)} %bitcast.21, ...), custom_call_target="tpu_custom_call" | custom-call | tf_op jit(solution)/shard_map/station_terms/pallas_call | solution.py:378
  1.9 8.3 %collective-permute-start.1 = (f32[64,128]{1,0:T(8,128)S(1)}, f32[64,128]{1,0:T(8,128)S(1)}, u32[]{:S(2)}, u32[]{:S(2)}) collective-permute-start(f32[64,128]{1,0:T(8,128)S(1)} %get-tuple-element.24.refs_0_.refs_4_), channel_id=1, source_target_pairs={{0,256},{16,272},{32,288},{48,304},{64,320},{80,336},{96,352},{112... | collective-permute-start | bytes 98312 | tf_op jit(solution)/shard_map/ppermute | solution.py:415
  10.2 3.1 %collective-permute-start = (f32[64,128]{1,0:T(8,128)S(1)}, f32[64,128]{1,0:T(8,128)S(1)}, u32[]{:S(2)}, u32[]{:S(2)}) collective-permute-start(f32[64,128]{1,0:T(8,128)S(1)} %get-tuple-element.24.refs_0_.refs_4_), channel_id=1, source_target_pairs={{0,16},{16,0},{32,48},{48,32},{64,80},{80,64},{96,112},{112,96},{1... | collective-permute-start | bytes 98312 | tf_op jit(solution)/shard_map/ppermute | solution.py:416
  13.3 6.8 %all-gather = f32[128,128]{1,0:T(8,128)S(1)} all-gather(f32[64,128]{1,0:T(8,128)S(1)} %get-tuple-element.24.refs_0_.refs_4_), channel_id=2, replica_groups={{16,32},{48,64},{80,96},{112,128},{144,160},{176,192},{208,224},{240,25..., dimensions={0}, use_global_device_ids=true | all-gather | bytes 98304 | tf_op jit(solution)/shard_map/all_gather | solution.py:417
  20.0 0.0 collective-permute-done.1.refs_3_
  20.1 0.0 collective-permute-done.refs_1_
  20.1 3.1 %baselines.1 = (f32[32,128]{1,0:T(8,128)S(1)}, f32[32,128]{1,0:T(8,128)S(1)}, f32[32,128]{1,0:T(8,128)S(1)}, f32[32,128]{1,0:T(8,128)S(1)}) custom-call(f32[64,128]{1,0:T(8,128)S(1)} %get-tuple-element.24.refs_0_.refs_4_, f32[64,128]{1,0:T(8,128)S(1)} %collective-permute-done.refs_1_, f32[2,64,128]{2,1,0:T(8,128)S(1)} %bitcast.16, ...), custom_call_target="tpu_custom_call" | custom-call | tf_op jit(solution)/shard_map/baselines/pallas_call | solution.py:420
  23.1 1.9 %collective-permute-start.2 = (f32[32,128]{1,0:T(8,128)S(1)}, f32[32,128]{1,0:T(8,128)S(1)}, u32[]{:S(2)}, u32[]{:S(2)}) collective-permute-start(f32[32,128]{1,0:T(8,128)S(1)} %get-tuple-element.29), channel_id=1, source_target_pairs={{0,16},{16,0},{32,48},{48,32},{64,80},{80,64},{96,112},{112,96},{1... | collective-permute-start | bytes 49160 | tf_op jit(solution)/shard_map/ppermute | solution.py:416
  25.0 1.9 %collective-permute-start.3 = (f32[32,128]{1,0:T(8,128)S(1)}, f32[32,128]{1,0:T(8,128)S(1)}, u32[]{:S(2)}, u32[]{:S(2)}) collective-permute-start(f32[32,128]{1,0:T(8,128)S(1)} %get-tuple-element.31), channel_id=1, source_target_pairs={{0,256},{16,272},{32,288},{48,304},{64,320},{80,336},{96,352},{112... | collective-permute-start | bytes 49160 | tf_op jit(solution)/shard_map/ppermute | solution.py:415
  27.0 0.0 copy-start
  27.0 0.0 copy-start.1
  27.0 6.6 %all-gather.1 = f32[64,128]{1,0:T(8,128)S(1)} all-gather(f32[32,128]{1,0:T(8,128)S(1)} %get-tuple-element.30), channel_id=3, replica_groups={{16,32},{48,64},{80,96},{112,128},{144,160},{176,192},{208,224},{240,25..., dimensions={0}, use_global_device_ids=true | all-gather | bytes 49152 | tf_op jit(solution)/shard_map/all_gather | solution.py:417
  33.6 0.0 collective-permute-done.2.refs_1_
  33.6 0.0 collective-permute-done.3.refs_3_
  33.6 0.0 copy-done
  33.6 0.0 copy-done.1
  33.6 0.2 curvature.1
  33.8 16.4 %all_to_all.17 = f32[8,1,128]{2,1,0:T(1,128)S(1)} all-to-all(f32[8,1,128]{2,1,0:T(1,128)S(1)} %bitcast.19), channel_id=1, replica_groups=mesh['base'=32,'z'=8,'core'=2] {'z'}, dimensions={0} | all-to-all | bytes 8192 | tf_op jit(solution)/shard_map/all_to_all | solution.py:447
  50.2 0.0 copy-start.2
  50.3 21.9 %all_to_all.18 = f32[64,1,128]{2,1,0:T(1,128)S(1)} all-to-all(f32[64,1,128]{2,1,0:T(1,128)S(1)} %broadcast_in_dim.2), channel_id=1, replica_groups=mesh['base'=32,'z'=8,'core'=2] {'base','core'}, dimensions={0} | all-to-all | bytes 65536 | tf_op jit(solution)/shard_map/all_to_all | solution.py:450
  72.1 0.0 copy-done.2
  72.1 0.8 %update.1 = (f32[4,8,128]{2,1,0:T(8,128)}, f32[2,4]{1,0:T(2,128)}, f32[4,8,128]{2,1,0:T(8,128)}, f32[2,4]{1,0:T(2,128)}, f32[4,8,128]{2,1,0:T(8,128)}, /*index=5*/f32[2,4]{1,0:T(2,128)}) custom-call(f32[64,128]{1,0:T(8,128)S(1)} %bitcast.18, f32[4,8,128]{2,1,0:T(8,128)S(1)} %get-tuple-element.35.curv_ref, ...), custom_call_target="tpu_custom_call" | custom-call | tf_op jit(solution)/shard_map/update/pallas_call | solution.py:452
  (2 shorter events, 0.0 us)
Async XLA Ops:
  1.9 18.2 %collective-permute-start.1 = (f32[64,128]{1,0:T(8,128)S(1)}, f32[64,128]{1,0:T(8,128)S(1)}, u32[]{:S(2)}, u32[]{:S(2)}) collective-permute-start(f32[64,128]{1,0:T(8,128)S(1)} %get-tuple-element.24.refs_0_.refs_4_), channel_id=1, source_target_pairs={{0,256},{16,272},{32,288},{48,304},{64,320},{80,336},{96,352},{112... | collective-permute-start | bytes 98312 | tf_op jit(solution)/shard_map/ppermute | solution.py:415
  10.2 9.9 %collective-permute-start = (f32[64,128]{1,0:T(8,128)S(1)}, f32[64,128]{1,0:T(8,128)S(1)}, u32[]{:S(2)}, u32[]{:S(2)}) collective-permute-start(f32[64,128]{1,0:T(8,128)S(1)} %get-tuple-element.24.refs_0_.refs_4_), channel_id=1, source_target_pairs={{0,16},{16,0},{32,48},{48,32},{64,80},{80,64},{96,112},{112,96},{1... | collective-permute-start | bytes 98312 | tf_op jit(solution)/shard_map/ppermute | solution.py:416
  23.1 10.5 %collective-permute-start.2 = (f32[32,128]{1,0:T(8,128)S(1)}, f32[32,128]{1,0:T(8,128)S(1)}, u32[]{:S(2)}, u32[]{:S(2)}) collective-permute-start(f32[32,128]{1,0:T(8,128)S(1)} %get-tuple-element.29), channel_id=1, source_target_pairs={{0,16},{16,0},{32,48},{48,32},{64,80},{80,64},{96,112},{112,96},{1... | collective-permute-start | bytes 49160 | tf_op jit(solution)/shard_map/ppermute | solution.py:416
  25.0 8.6 %collective-permute-start.3 = (f32[32,128]{1,0:T(8,128)S(1)}, f32[32,128]{1,0:T(8,128)S(1)}, u32[]{:S(2)}, u32[]{:S(2)}) collective-permute-start(f32[32,128]{1,0:T(8,128)S(1)} %get-tuple-element.31), channel_id=1, source_target_pairs={{0,256},{16,272},{32,288},{48,304},{64,320},{80,336},{96,352},{112... | collective-permute-start | bytes 49160 | tf_op jit(solution)/shard_map/ppermute | solution.py:415
  27.0 6.6 %copy-start = (f32[4,8,128]{2,1,0:T(8,128)S(1)}, f32[4,8,128]{2,1,0:T(8,128)}, u32[]{:S(2)}) copy-start(f32[4,8,128]{2,1,0:T(8,128)} %band_ref.1) | copy-start | bytes 49156
  27.0 6.6 %copy-start.1 = (f32[4,8,128]{2,1,0:T(8,128)S(1)}, f32[4,8,128]{2,1,0:T(8,128)}, u32[]{:S(2)}) copy-start(f32[4,8,128]{2,1,0:T(8,128)} %res_ref.1) | copy-start | bytes 49156
  50.2 21.9 %copy-start.2 = (f32[4,8,128]{2,1,0:T(8,128)S(1)}, f32[4,8,128]{2,1,0:T(8,128)}, u32[]{:S(2)}) copy-start(f32[4,8,128]{2,1,0:T(8,128)} %iter_ref.1) | copy-start | bytes 49156

commit v3 on v2

--- a/solution.py
+++ b/solution.py
@@ -78,6 +78,7 @@
     gains_ref, band_ref, delays_ref, ids, packed, sems, *, channels, blocks
 ):
     owned, _, width = gains_ref.shape
+    rows = ids.shape[1]
     half = 2 * owned
     pairs = [
         (first_hbm, ids.at[0:1]),
@@ -86,10 +87,13 @@
         (move_hbm, small_ref.at[0]),
         (gains_hbm, gains_ref),
         (band_hbm, band_ref),
-        (model_hbm, model_ref),
-        (left_hbm, small_ref.at[1]),
-        (iter_hbm, small_ref.at[2]),
     ]
+    parts = 1
+    share = 8 * rows // parts
+    for k in range(parts):
+        at = pl.ds(k * share, share)
+        pairs.append((model_hbm.at[at], model_ref.at[at]))
+    pairs += [(left_hbm, small_ref.at[1]), (iter_hbm, small_ref.at[2])]
     copies = [pltpu.make_async_copy(a, b, sems.at[k]) for k, (a, b) in enumerate(pairs)]
     for copy in copies:
         copy.start()
@@ -183,16 +187,15 @@
 
 def baseline_kernel(
     own_ref, even_ref, odd_ref, far_ref, model_ref, gather_ref, scatter_ref,
-    own_out, even_out, odd_out, far_out, table, picked, grads, model_parts, *, factor
+    own_out, far_out, even_out, odd_out, table, picked, grads, model_parts, *, factor
 ):
     _, rows, width = model_parts.shape
     slots = table.shape[0]
     owned = slots // 4
     group = 32
     size = 8 * group
-    pick, scatter = gather_ref[...], scatter_ref[...]
-    partner = odd_ref.at[lax.axis_index("base") % 2]
-    for k, ref in enumerate((own_ref, even_ref, partner, far_ref)):
+    partner = even_ref.at[1 - lax.axis_index("base") % 2]
+    for k, ref in enumerate((own_ref, partner, odd_ref, far_ref)):
         for j in range(16):
             table[k * owned : (k + 1) * owned, j * width : (j + 1) * width] = ref[
                 j * owned : (j + 1) * owned, :
@@ -205,25 +208,28 @@
     split = jnp.concatenate(
         [high, middle, low, jnp.zeros((128 - 3 * slots, exact.shape[1]), bf16)], axis=0
     )
-    step = 2 * width
-    for n in range(0, 16 * width, step):
-        picked[:, n : n + step] = jnp.dot(pick, split[:, n : n + step], preferred_element_type=f32)
-
     out_row = lax.broadcasted_iota(jnp.int32, (size, size), 0)
     in_row = lax.broadcasted_iota(jnp.int32, (size, size), 1)
     wanted = (out_row % group) * 8 + out_row // group
     shuffle = jnp.where(in_row == wanted, 1.0, 0.0).astype(bf16)
-    for g in range(rows // group):
-        part = jnp.dot(
-            shuffle, model_ref[g * size : (g + 1) * size, :], preferred_element_type=f32
-        )
-        for j in range(8):
-            model_parts[j, g * group : (g + 1) * group, :] = part[j * group : (j + 1) * group, :]
-
-    def chunk(i, carry):
-        at = pl.ds(pl.multiple_of(i * 8, 8), 8)
-        at_q = pl.ds(pl.multiple_of(rows + i * 8, 8), 8)
-        cols = [slice(j * width, (j + 1) * width) for j in range(16)]
+    step = 2 * width
+    cols = [slice(j * width, (j + 1) * width) for j in range(16)]
+    stage = rows // 2
+    def load(first):
+        for g in range(first // group, (first + stage) // group):
+            part = jnp.dot(
+                shuffle, model_ref[g * size : (g + 1) * size, :], preferred_element_type=f32
+            )
+            for j in range(8):
+                model_parts[j, g * group : (g + 1) * group, :] = part[j * group : (j + 1) * group, :]
+        for base in (first, rows + first):
+            pick = gather_ref[base : base + stage, :]
+            for n in range(0, 16 * width, step):
+                picked[base : base + stage, n : n + step] = jnp.dot(pick, split[:, n : n + step], preferred_element_type=f32)
+
+    def chunk(i):
+        at = slice(i * 8, i * 8 + 8)
+        at_q = slice(rows + i * 8, rows + i * 8 + 8)
         model = [model_parts[j, at, :] for j in range(8)]
         right = times_adjoint(model, [picked[at_q, c] for c in cols[:8]])
         left = times([picked[at, c] for c in cols[:8]], model)
@@ -234,18 +240,31 @@
             grads[at, c] = value
         for c, value in zip(cols, adjoint_times(change, left)):
             grads[at_q, c] = value
-        return carry
-
-    lax.fori_loop(0, rows // 8, chunk, 0, unroll=2)
-    sums = []
-    for n in range(0, 8 * width, step):
-        value = grads[:, n : n + step]
-        high = value.astype(bf16)
-        low = (value - high.astype(f32)).astype(bf16)
-        total = jnp.dot(scatter, high, preferred_element_type=f32) + jnp.dot(
-            scatter, low, preferred_element_type=f32
-        )
-        table[:, n : n + step] = factor * total
+
+    def collect(first):
+        for n in range(0, 8 * width, step):
+            total = None
+            for base in (first, rows + first):
+                value = grads[base : base + stage, n : n + step]
+                sel = scatter_ref[:, base : base + stage]
+                high = value.astype(bf16)
+                low = (value - high.astype(f32)).astype(bf16)
+                part = jnp.dot(sel, high, preferred_element_type=f32) + jnp.dot(
+                    sel, low, preferred_element_type=f32
+                )
+                total = part if total is None else total + part
+            if first:
+                table[:, n : n + step] = table[:, n : n + step] + factor * total
+            else:
+                table[:, n : n + step] = factor * total
+
+    load(0)
+    for first in range(0, rows, stage):
+        if first + stage < rows:
+            load(first + stage)
+        for i in range(first // 8, (first + stage) // 8):
+            chunk(i)
+        collect(first)
     for k, ref in enumerate((own_out, even_out, odd_out, far_out)):
         for j in range(8):
             ref[j * owned : (j + 1) * owned, :] = table[
@@ -254,7 +273,7 @@
 
 
 def curvature_kernel(
-    own_ref, even_ref, odd_ref, far_ref, terms_ref, turn_ref, small_ref, band_ref, res_ref,
+    own_ref, far_ref, even_ref, odd_ref, terms_ref, turn_ref, small_ref, band_ref, res_ref,
     curv_ref, row_ref, *, channels
 ):
     owned, _, width = band_ref.shape
@@ -263,7 +282,7 @@
     freq = frequencies(chan_index(), width, channels)
     cosine = turn_ref[0:half, :]
     sine = turn_ref[half : 2 * half, :]
-    total = own_ref[...] + even_ref[...] + odd_ref[lax.axis_index("base") % 2] + far_ref[...]
+    total = own_ref[...] + even_ref[1 - lax.axis_index("base") % 2] + odd_ref[...] + far_ref[...]
     moved = jnp.zeros((half, width), f32)
     for r in range(2):
         re = slice(r * half, (r + 1) * half)
@@ -408,16 +427,16 @@
     )
 
     far_pairs = [(i, (i + blocks // 2) % blocks) for i in range(blocks)]
-    even_pairs = [(i, i ^ 1) for i in range(blocks)]
-    odd_groups = [[i, (i + 1) % blocks] for i in range(1, blocks, 2)]
+    odd_pairs = [(i, (i + 1) % blocks if i % 2 else (i - 1) % blocks) for i in range(blocks)]
+    even_groups = [[i, i + 1] for i in range(0, blocks, 2)]
 
     def exchange(to_even, to_odd, to_far):
         far = lax.ppermute(to_far, "base", far_pairs)
-        even = lax.ppermute(to_even, "base", even_pairs)
-        odd = lax.all_gather(to_odd, "base", axis_index_groups=odd_groups)
+        odd = lax.ppermute(to_odd, "base", odd_pairs)
+        even = lax.all_gather(to_even, "base", axis_index_groups=even_groups)
         return even, odd, far
 
-    own, to_even, to_odd, to_far = pl.pallas_call(
+    own, to_far, to_even, to_odd = pl.pallas_call(
         lambda *refs: baseline_kernel(*refs, factor=factor),
         out_shape=(shape(8 * owned, width),) * 4,
         in_specs=[vmem()] * 7,
@@ -435,6 +454,7 @@
         model_local, gather, scatter,
     )
 
+    from_even, from_odd, from_far = exchange(to_even, to_odd, to_far)
     curv, row = pl.pallas_call(
         lambda *refs: curvature_kernel(*refs, channels=channels),
         out_shape=(shape(owned, 8, width), shape(lines, width)),
@@ -442,7 +462,7 @@
         out_specs=(vmem(), vmem()),
         compiler_params=params(4),
         name="curvature",
-    )(own, *exchange(to_even, to_odd, to_far), terms, turn, small, dir_band, res_band)
+    )(own, from_far, from_even, from_odd, terms, turn, small, dir_band, res_band)
 
     line = lax.all_to_all(row, "z", 0, 0, tiled=True)
     peers = blocks * cores

time: 73.3 us -> 71 us (0.969)
  blocking collectives: 51.6 us -> 43.4 us
  starting transfers between devices: 15.3 us -> 21.6 us
    all_gather x2, blocking collectives: 13.4 us -> 6.9 us  [exchange(): even = lax.all_gather(to_even, 'base', axis_index_groups=even_groups)]
    ppermute x2, starting transfers between devices: 5.04 us -> 8.79 us  [exchange(): odd = lax.ppermute(to_odd, 'base', odd_pairs)]
    ppermute x2, starting transfers between devices: 10.2 us -> 12.8 us  [exchange(): far = lax.ppermute(to_far, 'base', far_pairs)]
    all_to_all x1, blocking collectives: 21.9 us -> 20.1 us  [body(): everyone = lax.all_to_all(line, ('base', 'core'), 0, 0, tiled=True)]
  transfers between devices with their start and end apart: 4 -> 4, of which waited for: 0 -> 1; matrix products, arithmetic and copies ran while one was open for 0% -> 0% of each run, Pallas kernels for 0% -> 0%
where the time goes in v3:
time: 71 us; the launch traced here: 70.6 us
  blocking collectives  43.4 us (61%)
  starting transfers between devices  21.6 us (30%)
  Pallas kernels  4.75 us (7%)
  between operations  0.73 us (1%)
    all_to_all x1, blocking collectives, body(): everyone = lax.all_to_all(line, ('base', 'core'), 0, 0, tiled=True)  20.1 us
    all_to_all x1, blocking collectives, body(): line = lax.all_to_all(row, 'z', 0, 0, tiled=True)  16.4 us
    ppermute x2, starting transfers between devices, exchange(): far = lax.ppermute(to_far, 'base', far_pairs)  12.8 us
    ppermute x2, starting transfers between devices, exchange(): odd = lax.ppermute(to_odd, 'base', odd_pairs)  8.79 us
    all_gather x2, blocking collectives, exchange(): even = lax.all_gather(to_even, 'base', axis_index_groups=even_groups)  6.9 us
    pallas_call x1, Pallas kernels, body(): pl.pallas_call(lambda *refs: baseline_kernel(*refs, factor=factor), out_s...  2.52 us
  transfers between devices with their start and end apart: 4, of which 1 were waited for; matrix products, arithmetic and copies ran while one was open for 0% of the time, Pallas kernels for 0%

profile of v3, /device:TPU:1, one launch (start us, length us, event | category | flops | bytes accessed | tf_op | source)
XLA Modules:
  0.0 70.6 jit_solution(6204176112169410652)
XLA Ops:
  0.6 1.2 %station_terms.1 = (f32[64,128]{1,0:T(8,128)S(1)}, f32[16,128]{1,0:T(8,128)S(1)}, f32[3,2,4]{2,1,0:T(2,128)S(1)}, bf16[512,128]{1,0:T(8,128)(2,1)S(1)}, bf16[16,...) custom-call(f32[4,8,128]{2,1,0:T(8,128)} %refs_0_.1, f32[4,8,128]{2,1,0:T(8,128)} %band_ref.1, f32[2,4]{1,0:T(2,128)} %bitcast.21, ...), custom_call_target="tpu_custom_call" | custom-call | tf_op jit(solution)/shard_map/station_terms/pallas_call | solution.py:397
  1.9 8.3 %collective-permute-start.1 = (f32[64,128]{1,0:T(8,128)S(1)}, f32[64,128]{1,0:T(8,128)S(1)}, u32[]{:S(2)}, u32[]{:S(2)}) collective-permute-start(f32[64,128]{1,0:T(8,128)S(1)} %get-tuple-element.24.refs_0_.refs_4_), channel_id=1, source_target_pairs={{0,256},{16,272},{32,288},{48,304},{64,320},{80,336},{96,352},{112... | collective-permute-start | bytes 98312 | tf_op jit(solution)/shard_map/ppermute | solution.py:434
  10.2 4.3 %collective-permute-start = (f32[64,128]{1,0:T(8,128)S(1)}, f32[64,128]{1,0:T(8,128)S(1)}, u32[]{:S(2)}, u32[]{:S(2)}) collective-permute-start(f32[64,128]{1,0:T(8,128)S(1)} %get-tuple-element.24.refs_0_.refs_4_), channel_id=1, source_target_pairs={{0,496},{16,32},{32,16},{48,64},{64,48},{80,96},{96,80},{112,128},... | collective-permute-start | bytes 98312 | tf_op jit(solution)/shard_map/ppermute | solution.py:435
  14.4 3.6 %all-gather = f32[128,128]{1,0:T(8,128)S(1)} all-gather(f32[64,128]{1,0:T(8,128)S(1)} %get-tuple-element.24.refs_0_.refs_4_), channel_id=2, replica_groups={{0,16},{32,48},{64,80},{96,112},{128,144},{160,176},{192,208},{224,240}..., dimensions={0}, use_global_device_ids=true | all-gather | bytes 98304 | tf_op jit(solution)/shard_map/all_gather | solution.py:436
  18.1 0.0 collective-permute-done.1.refs_3_
  18.1 0.1 collective-permute-done.refs_2_
  18.1 2.5 %baselines.1 = (f32[32,128]{1,0:T(8,128)S(1)}, f32[32,128]{1,0:T(8,128)S(1)}, f32[32,128]{1,0:T(8,128)S(1)}, f32[32,128]{1,0:T(8,128)S(1)}) custom-call(f32[64,128]{1,0:T(8,128)S(1)} %get-tuple-element.24.refs_0_.refs_4_, f32[2,64,128]{2,1,0:T(8,128)S(1)} %bitcast.16, f32[64,128]{1,0:T(8,128)S(1)} %collective-permute-done.refs_2_, ...), custom_call_target="tpu_custom_call" | custom-call | tf_op jit(solution)/shard_map/baselines/pallas_call | solution.py:439
  20.7 4.5 %collective-permute-start.2 = (f32[32,128]{1,0:T(8,128)S(1)}, f32[32,128]{1,0:T(8,128)S(1)}, u32[]{:S(2)}, u32[]{:S(2)}) collective-permute-start(f32[32,128]{1,0:T(8,128)S(1)} %get-tuple-element.29), channel_id=1, source_target_pairs={{0,256},{16,272},{32,288},{48,304},{64,320},{80,336},{96,352},{112... | collective-permute-start | bytes 49160 | tf_op jit(solution)/shard_map/ppermute | solution.py:434
  25.2 4.5 %collective-permute-start.3 = (f32[32,128]{1,0:T(8,128)S(1)}, f32[32,128]{1,0:T(8,128)S(1)}, u32[]{:S(2)}, u32[]{:S(2)}) collective-permute-start(f32[32,128]{1,0:T(8,128)S(1)} %get-tuple-element.31), channel_id=1, source_target_pairs={{0,496},{16,32},{32,16},{48,64},{64,48},{80,96},{96,80},{112,128},... | collective-permute-start | bytes 49160 | tf_op jit(solution)/shard_map/ppermute | solution.py:435
  29.7 0.0 copy-start
  29.7 0.0 copy-start.1
  29.7 3.3 %all-gather.1 = f32[64,128]{1,0:T(8,128)S(1)} all-gather(f32[32,128]{1,0:T(8,128)S(1)} %get-tuple-element.30), channel_id=3, replica_groups={{0,16},{32,48},{64,80},{96,112},{128,144},{160,176},{192,208},{224,240}..., dimensions={0}, use_global_device_ids=true | all-gather | bytes 49152 | tf_op jit(solution)/shard_map/all_gather | solution.py:436
  33.0 0.0 collective-permute-done.2.refs_1_
  33.0 0.0 collective-permute-done.3.refs_3_
  33.0 0.0 copy-done
  33.0 0.0 copy-done.1
  33.0 0.2 curvature.1
  33.2 16.4 %all_to_all.17 = f32[8,1,128]{2,1,0:T(1,128)S(1)} all-to-all(f32[8,1,128]{2,1,0:T(1,128)S(1)} %bitcast.19), channel_id=1, replica_groups=mesh['base'=32,'z'=8,'core'=2] {'z'}, dimensions={0} | all-to-all | bytes 8192 | tf_op jit(solution)/shard_map/all_to_all | solution.py:467
  49.6 0.0 copy-start.2
  49.7 20.1 %all_to_all.18 = f32[64,1,128]{2,1,0:T(1,128)S(1)} all-to-all(f32[64,1,128]{2,1,0:T(1,128)S(1)} %broadcast_in_dim.2), channel_id=1, replica_groups=mesh['base'=32,'z'=8,'core'=2] {'base','core'}, dimensions={0} | all-to-all | bytes 65536 | tf_op jit(solution)/shard_map/all_to_all | solution.py:470
  69.8 0.0 copy-done.2
  69.8 0.8 %update.1 = (f32[4,8,128]{2,1,0:T(8,128)}, f32[2,4]{1,0:T(2,128)}, f32[4,8,128]{2,1,0:T(8,128)}, f32[2,4]{1,0:T(2,128)}, f32[4,8,128]{2,1,0:T(8,128)}, /*index=5*/f32[2,4]{1,0:T(2,128)}) custom-call(f32[64,128]{1,0:T(8,128)S(1)} %bitcast.18, f32[4,8,128]{2,1,0:T(8,128)S(1)} %get-tuple-element.35.curv_ref, ...), custom_call_target="tpu_custom_call" | custom-call | tf_op jit(solution)/shard_map/update/pallas_call | solution.py:472
  (2 shorter events, 0.0 us)
Async XLA Ops:
  1.9 16.2 %collective-permute-start.1 = (f32[64,128]{1,0:T(8,128)S(1)}, f32[64,128]{1,0:T(8,128)S(1)}, u32[]{:S(2)}, u32[]{:S(2)}) collective-permute-start(f32[64,128]{1,0:T(8,128)S(1)} %get-tuple-element.24.refs_0_.refs_4_), channel_id=1, source_target_pairs={{0,256},{16,272},{32,288},{48,304},{64,320},{80,336},{96,352},{112... | collective-permute-start | bytes 98312 | tf_op jit(solution)/shard_map/ppermute | solution.py:434
  10.2 8.0 %collective-permute-start = (f32[64,128]{1,0:T(8,128)S(1)}, f32[64,128]{1,0:T(8,128)S(1)}, u32[]{:S(2)}, u32[]{:S(2)}) collective-permute-start(f32[64,128]{1,0:T(8,128)S(1)} %get-tuple-element.24.refs_0_.refs_4_), channel_id=1, source_target_pairs={{0,496},{16,32},{32,16},{48,64},{64,48},{80,96},{96,80},{112,128},... | collective-permute-start | bytes 98312 | tf_op jit(solution)/shard_map/ppermute | solution.py:435
  20.7 12.3 %collective-permute-start.2 = (f32[32,128]{1,0:T(8,128)S(1)}, f32[32,128]{1,0:T(8,128)S(1)}, u32[]{:S(2)}, u32[]{:S(2)}) collective-permute-start(f32[32,128]{1,0:T(8,128)S(1)} %get-tuple-element.29), channel_id=1, source_target_pairs={{0,256},{16,272},{32,288},{48,304},{64,320},{80,336},{96,352},{112... | collective-permute-start | bytes 49160 | tf_op jit(solution)/shard_map/ppermute | solution.py:434
  25.2 7.8 %collective-permute-start.3 = (f32[32,128]{1,0:T(8,128)S(1)}, f32[32,128]{1,0:T(8,128)S(1)}, u32[]{:S(2)}, u32[]{:S(2)}) collective-permute-start(f32[32,128]{1,0:T(8,128)S(1)} %get-tuple-element.31), channel_id=1, source_target_pairs={{0,496},{16,32},{32,16},{48,64},{64,48},{80,96},{96,80},{112,128},... | collective-permute-start | bytes 49160 | tf_op jit(solution)/shard_map/ppermute | solution.py:435
  29.7 3.3 %copy-start = (f32[4,8,128]{2,1,0:T(8,128)S(1)}, f32[4,8,128]{2,1,0:T(8,128)}, u32[]{:S(2)}) copy-start(f32[4,8,128]{2,1,0:T(8,128)} %band_ref.1) | copy-start | bytes 49156
  29.7 3.3 %copy-start.1 = (f32[4,8,128]{2,1,0:T(8,128)S(1)}, f32[4,8,128]{2,1,0:T(8,128)}, u32[]{:S(2)}) copy-start(f32[4,8,128]{2,1,0:T(8,128)} %res_ref.1) | copy-start | bytes 49156
  49.6 20.1 %copy-start.2 = (f32[4,8,128]{2,1,0:T(8,128)S(1)}, f32[4,8,128]{2,1,0:T(8,128)}, u32[]{:S(2)}) copy-start(f32[4,8,128]{2,1,0:T(8,128)} %iter_ref.1) | copy-start | bytes 49156

commit v4 on v3

--- a/solution.py
+++ b/solution.py
@@ -29,6 +29,12 @@
 
 def shape(*dims, dtype=f32):
     return jax.ShapeDtypeStruct(dims, dtype)
+
+
+def group_place(blocks):
+    block = lax.axis_index("base")
+    first = jnp.where(block % 2 == 1, block, (block + blocks - 1) % blocks)
+    return 1 - block % 2 + 2 * jnp.where(first >= blocks // 2, 1, 0)
 
 
 def chan_index():
@@ -187,15 +193,19 @@
 
 def baseline_kernel(
     own_ref, even_ref, odd_ref, far_ref, model_ref, gather_ref, scatter_ref,
-    own_out, far_out, even_out, odd_out, table, picked, grads, model_parts, *, factor
+    even_out, group_out, table, picked, grads, model_parts, *, factor, blocks
 ):
     _, rows, width = model_parts.shape
     slots = table.shape[0]
     owned = slots // 4
     group = 32
     size = 8 * group
+    place = group_place(blocks)
+    odd_place = place + 1 - 2 * (place % 2)
+    far_place = (place + 2) % 4
     partner = even_ref.at[1 - lax.axis_index("base") % 2]
-    for k, ref in enumerate((own_ref, partner, odd_ref, far_ref)):
+    sources = (own_ref, partner, odd_ref, far_ref)
+    for k, ref in enumerate(sources):
         for j in range(16):
             table[k * owned : (k + 1) * owned, j * width : (j + 1) * width] = ref[
                 j * owned : (j + 1) * owned, :
@@ -265,7 +275,9 @@
         for i in range(first // 8, (first + stage) // 8):
             chunk(i)
         collect(first)
-    for k, ref in enumerate((own_out, even_out, odd_out, far_out)):
+    group_out[(odd_place + 2) % 4] = jnp.zeros(even_out.shape, f32)
+    sinks = (group_out.at[place], even_out, group_out.at[odd_place], group_out.at[far_place])
+    for k, ref in enumerate(sinks):
         for j in range(8):
             ref[j * owned : (j + 1) * owned, :] = table[
                 k * owned : (k + 1) * owned, j * width : (j + 1) * width
@@ -273,7 +285,7 @@
 
 
 def curvature_kernel(
-    own_ref, far_ref, even_ref, odd_ref, terms_ref, turn_ref, small_ref, band_ref, res_ref,
+    even_ref, group_ref, terms_ref, turn_ref, small_ref, band_ref, res_ref,
     curv_ref, row_ref, *, channels
 ):
     owned, _, width = band_ref.shape
@@ -282,7 +294,9 @@
     freq = frequencies(chan_index(), width, channels)
     cosine = turn_ref[0:half, :]
     sine = turn_ref[half : 2 * half, :]
-    total = own_ref[...] + even_ref[1 - lax.axis_index("base") % 2] + odd_ref[...] + far_ref[...]
+    total = even_ref[1 - lax.axis_index("base") % 2]
+    for k in range(4):
+        total = total + group_ref[k]
     moved = jnp.zeros((half, width), f32)
     for r in range(2):
         re = slice(r * half, (r + 1) * half)
@@ -426,21 +440,29 @@
         )
     )
 
-    far_pairs = [(i, (i + blocks // 2) % blocks) for i in range(blocks)]
+    even_groups = [[i, i + 1] for i in range(0, blocks, 2)]
+    half = blocks // 2
+    groups = [[i, i + 1, i + half, (i + 1 + half) % blocks] for i in range(1, half, 2)]
+
+    def exchange(to_even, to_group):
+        count = to_group.shape[1]
+        group = lax.all_to_all(
+            to_group.reshape(4 * count, width), "base", 0, 0, axis_index_groups=groups, tiled=True
+        )
+        even = lax.all_gather(to_even, "base", axis_index_groups=even_groups)
+        return even, group.reshape(4, count, width)
+
+    far_pairs = [(i, (i + half) % blocks) for i in range(blocks)]
     odd_pairs = [(i, (i + 1) % blocks if i % 2 else (i - 1) % blocks) for i in range(blocks)]
-    even_groups = [[i, i + 1] for i in range(0, blocks, 2)]
-
-    def exchange(to_even, to_odd, to_far):
-        far = lax.ppermute(to_far, "base", far_pairs)
-        odd = lax.ppermute(to_odd, "base", odd_pairs)
-        even = lax.all_gather(to_even, "base", axis_index_groups=even_groups)
-        return even, odd, far
-
-    own, to_far, to_even, to_odd = pl.pallas_call(
-        lambda *refs: baseline_kernel(*refs, factor=factor),
-        out_shape=(shape(8 * owned, width),) * 4,
+    from_far = lax.ppermute(terms, "base", far_pairs)
+    from_odd = lax.ppermute(terms, "base", odd_pairs)
+    from_even = lax.all_gather(terms, "base", axis_index_groups=even_groups)
+
+    to_even, to_group = pl.pallas_call(
+        lambda *refs: baseline_kernel(*refs, factor=factor, blocks=blocks),
+        out_shape=(shape(8 * owned, width), shape(4, 8 * owned, width)),
         in_specs=[vmem()] * 7,
-        out_specs=(vmem(),) * 4,
+        out_specs=(vmem(),) * 2,
         scratch_shapes=[
             pltpu.VMEM((slots, 16 * width), f32),
             pltpu.VMEM((2 * rows, 16 * width), f32),
@@ -449,20 +471,16 @@
         ],
         compiler_params=params(24),
         name="baselines",
-    )(
-        terms, *exchange(terms, terms, terms),
-        model_local, gather, scatter,
-    )
-
-    from_even, from_odd, from_far = exchange(to_even, to_odd, to_far)
+    )(terms, from_even, from_odd, from_far, model_local, gather, scatter)
+
     curv, row = pl.pallas_call(
         lambda *refs: curvature_kernel(*refs, channels=channels),
         out_shape=(shape(owned, 8, width), shape(lines, width)),
-        in_specs=[vmem()] * 9,
+        in_specs=[vmem()] * 7,
         out_specs=(vmem(), vmem()),
         compiler_params=params(4),
         name="curvature",
-    )(own, from_far, from_even, from_odd, terms, turn, small, dir_band, res_band)
+    )(*exchange(to_even, to_group), terms, turn, small, dir_band, res_band)
 
     line = lax.all_to_all(row, "z", 0, 0, tiled=True)
     peers = blocks * cores

time: 71 us -> 69.5 us (0.979)
  starting transfers between devices: 21.6 us -> 19.3 us
  waiting for transfers between devices: 0.07 us -> 0.96 us
    ppermute x4 -> x2, starting transfers between devices: 21.6 us -> 12.6 us  [the longest x1 8.28 us: body(): from_far = lax.ppermute(terms, 'base', far_pairs)]
    all_to_all x0 -> x1, starting transfers between devices: none -> 6.72 us  [exchange(): lax.all_to_all(to_group.reshape(4 * count, width), 'base', 0, 0, axis_ind...]
    all_gather x0 -> x1, blocking collectives: none -> 3.63 us  [body(): from_even = lax.all_gather(terms, 'base', axis_index_groups=even_groups)]
    all_gather x2 -> x1, blocking collectives: 6.9 us -> 3.38 us  [exchange(): even = lax.all_gather(to_even, 'base', axis_index_groups=even_groups)]
    all_to_all x0 -> x1, waiting for transfers between devices: none -> 0.89 us  [exchange(): lax.all_to_all(to_group.reshape(4 * count, width), 'base', 0, 0, axis_ind...]
    all_to_all x1, blocking collectives: 20.1 us -> 19.4 us  [body(): everyone = lax.all_to_all(line, ('base', 'core'), 0, 0, tiled=True)]
  transfers between devices with their start and end apart: 4 -> 3, of which waited for: 1 -> 2; matrix products, arithmetic and copies ran while one was open for 0% -> 0% of each run, Pallas kernels for 0% -> 0%
where the time goes in v4:
time: 69.5 us; the launch traced here: 69.1 us
  blocking collectives  42.8 us (62%)
  starting transfers between devices  19.3 us (28%)
  Pallas kernels  5.38 us (8%)
  waiting for transfers between devices  0.96 us (1%)
    all_to_all x1, blocking collectives, body(): everyone = lax.all_to_all(line, ('base', 'core'), 0, 0, tiled=True)  19.4 us
    all_to_all x1, blocking collectives, body(): line = lax.all_to_all(row, 'z', 0, 0, tiled=True)  16.4 us
    ppermute x1, starting transfers between devices, body(): from_far = lax.ppermute(terms, 'base', far_pairs)  8.28 us
    all_to_all x1, starting transfers between devices, exchange(): lax.all_to_all(to_group.reshape(4 * count, width), 'base', 0, 0, axis_ind...  6.72 us
    ppermute x1, starting transfers between devices, body(): from_odd = lax.ppermute(terms, 'base', odd_pairs)  4.27 us
    all_gather x1, blocking collectives, body(): from_even = lax.all_gather(terms, 'base', axis_index_groups=even_groups)  3.63 us
    all_gather x1, blocking collectives, exchange(): even = lax.all_gather(to_even, 'base', axis_index_groups=even_groups)  3.38 us
    pallas_call x1, Pallas kernels, body(): pl.pallas_call(lambda *refs: baseline_kernel(*refs, factor=factor, blocks...  3.15 us
  transfers between devices with their start and end apart: 3, of which 2 were waited for; matrix products, arithmetic and copies ran while one was open for 0% of the time, Pallas kernels for 0%

profile of v4, /device:TPU:1, one launch (start us, length us, event | category | flops | bytes accessed | tf_op | source)
XLA Modules:
  0.0 69.1 jit_solution(14359010909965584607)
XLA Ops:
  0.6 1.2 %station_terms.1 = (f32[64,128]{1,0:T(8,128)S(1)}, f32[16,128]{1,0:T(8,128)S(1)}, f32[3,2,4]{2,1,0:T(2,128)S(1)}, bf16[512,128]{1,0:T(8,128)(2,1)S(1)}, bf16[16,...) custom-call(f32[4,8,128]{2,1,0:T(8,128)} %refs_0_.1, f32[4,8,128]{2,1,0:T(8,128)} %band_ref.1, f32[2,4]{1,0:T(2,128)} %bitcast.21, ...), custom_call_target="tpu_custom_call" | custom-call | tf_op jit(solution)/shard_map/station_terms/pallas_call | solution.py:411
  1.9 8.3 %collective-permute-start.1 = (f32[64,128]{1,0:T(8,128)S(1)}, f32[64,128]{1,0:T(8,128)S(1)}, u32[]{:S(2)}, u32[]{:S(2)}) collective-permute-start(f32[64,128]{1,0:T(8,128)S(1)} %get-tuple-element.22.refs_0_.refs_2_), channel_id=1, source_target_pairs={{0,256},{16,272},{32,288},{48,304},{64,320},{80,336},{96,352},{112... | collective-permute-start | bytes 98312 | tf_op jit(solution)/shard_map/ppermute | solution.py:457
  10.2 4.3 %collective-permute-start = (f32[64,128]{1,0:T(8,128)S(1)}, f32[64,128]{1,0:T(8,128)S(1)}, u32[]{:S(2)}, u32[]{:S(2)}) collective-permute-start(f32[64,128]{1,0:T(8,128)S(1)} %get-tuple-element.22.refs_0_.refs_2_), channel_id=1, source_target_pairs={{0,496},{16,32},{32,16},{48,64},{64,48},{80,96},{96,80},{112,128},... | collective-permute-start | bytes 98312 | tf_op jit(solution)/shard_map/ppermute | solution.py:458
  14.4 3.6 %all-gather = f32[128,128]{1,0:T(8,128)S(1)} all-gather(f32[64,128]{1,0:T(8,128)S(1)} %get-tuple-element.22.refs_0_.refs_2_), channel_id=2, replica_groups={{0,16},{32,48},{64,80},{96,112},{128,144},{160,176},{192,208},{224,240}..., dimensions={0}, use_global_device_ids=true | all-gather | bytes 98304 | tf_op jit(solution)/shard_map/all_gather | solution.py:459
  18.1 0.0 collective-permute-done.1.refs_3_
  18.1 0.1 collective-permute-done.refs_2_
  18.1 3.2 %baselines.1 = (f32[32,128]{1,0:T(8,128)S(1)}, f32[4,32,128]{2,1,0:T(8,128)}) custom-call(f32[64,128]{1,0:T(8,128)S(1)} %get-tuple-element.22.refs_0_.refs_2_, f32[2,64,128]{2,1,0:T(8,128)S(1)} %bitcast.16, f32[64,128]{1,0:T(8,128)S(1)} %collective-permute-done.refs_2_, f32[64,128]{1,0:T(8,128)S(1)} %collective-permute-done.1.refs_3_, ...), custom_call_target="tpu_custom_call" | custom-call | tf_op jit(solution)/shard_map/baselines/pallas_call | solution.py:461
  21.3 6.7 %all-to-all-start = ((f32[4,32,128]{2,1,0:T(8,128)}), f32[4,32,128]{2,1,0:T(8,128)S(1)}, u32[]{:S(2)}, u32[]{:S(2)}) async-start(f32[4,32,128]{2,1,0:T(8,128)} %get-tuple-element.27), calls=%async_computation | async-start | bytes 131072 | tf_op jit(solution)/shard_map/all_to_all | solution.py:449
  28.0 0.0 copy-start
  28.0 0.0 copy-start.1
  28.0 3.4 %all-gather.1 = f32[64,128]{1,0:T(8,128)S(1)} all-gather(f32[32,128]{1,0:T(8,128)S(1)} %get-tuple-element.26), channel_id=3, replica_groups={{0,16},{32,48},{64,80},{96,112},{128,144},{160,176},{192,208},{224,240}..., dimensions={0}, use_global_device_ids=true | all-gather | bytes 49152 | tf_op jit(solution)/shard_map/all_gather | solution.py:452
  31.4 0.9 %all-to-all-done.refs_1_ = f32[4,32,128]{2,1,0:T(8,128)S(1)} async-done(((f32[4,32,128]{2,1,0:T(8,128)}), f32[4,32,128]{2,1,0:T(8,128)S(1)}, u32[]{:S(2)}, u32[]{:S(2)}) %all-to-all-start) | async-done | bytes 65568 | tf_op jit(solution)/shard_map/all_to_all | solution.py:449
  32.3 0.0 copy-done
  32.3 0.0 copy-done.1
  32.3 0.2 curvature.1
  32.5 16.4 %all_to_all.23 = f32[8,1,128]{2,1,0:T(1,128)S(1)} all-to-all(f32[8,1,128]{2,1,0:T(1,128)S(1)} %bitcast.19), channel_id=1, replica_groups=mesh['base'=32,'z'=8,'core'=2] {'z'}, dimensions={0} | all-to-all | bytes 8192 | tf_op jit(solution)/shard_map/all_to_all | solution.py:485
  48.9 0.0 copy-start.2
  48.9 19.4 %all_to_all.24 = f32[64,1,128]{2,1,0:T(1,128)S(1)} all-to-all(f32[64,1,128]{2,1,0:T(1,128)S(1)} %broadcast_in_dim.2), channel_id=1, replica_groups=mesh['base'=32,'z'=8,'core'=2] {'base','core'}, dimensions={0} | all-to-all | bytes 65536 | tf_op jit(solution)/shard_map/all_to_all | solution.py:488
  68.3 0.0 copy-done.2
  68.3 0.8 %update.1 = (f32[4,8,128]{2,1,0:T(8,128)}, f32[2,4]{1,0:T(2,128)}, f32[4,8,128]{2,1,0:T(8,128)}, f32[2,4]{1,0:T(2,128)}, f32[4,8,128]{2,1,0:T(8,128)}, /*index=5*/f32[2,4]{1,0:T(2,128)}) custom-call(f32[64,128]{1,0:T(8,128)S(1)} %bitcast.17, f32[4,8,128]{2,1,0:T(8,128)S(1)} %get-tuple-element.31.curv_ref, ...), custom_call_target="tpu_custom_call" | custom-call | tf_op jit(solution)/shard_map/update/pallas_call | solution.py:490
  (2 shorter events, 0.0 us)
Async XLA Ops:
  1.9 16.2 %collective-permute-start.1 = (f32[64,128]{1,0:T(8,128)S(1)}, f32[64,128]{1,0:T(8,128)S(1)}, u32[]{:S(2)}, u32[]{:S(2)}) collective-permute-start(f32[64,128]{1,0:T(8,128)S(1)} %get-tuple-element.22.refs_0_.refs_2_), channel_id=1, source_target_pairs={{0,256},{16,272},{32,288},{48,304},{64,320},{80,336},{96,352},{112... | collective-permute-start | bytes 98312 | tf_op jit(solution)/shard_map/ppermute | solution.py:457
  10.2 8.0 %collective-permute-start = (f32[64,128]{1,0:T(8,128)S(1)}, f32[64,128]{1,0:T(8,128)S(1)}, u32[]{:S(2)}, u32[]{:S(2)}) collective-permute-start(f32[64,128]{1,0:T(8,128)S(1)} %get-tuple-element.22.refs_0_.refs_2_), channel_id=1, source_target_pairs={{0,496},{16,32},{32,16},{48,64},{64,48},{80,96},{96,80},{112,128},... | collective-permute-start | bytes 98312 | tf_op jit(solution)/shard_map/ppermute | solution.py:458
  21.3 11.0 %all-to-all-start = ((f32[4,32,128]{2,1,0:T(8,128)}), f32[4,32,128]{2,1,0:T(8,128)S(1)}, u32[]{:S(2)}, u32[]{:S(2)}) async-start(f32[4,32,128]{2,1,0:T(8,128)} %get-tuple-element.27), calls=%async_computation | async-start | bytes 131072 | tf_op jit(solution)/shard_map/all_to_all | solution.py:449
  28.0 4.3 %copy-start = (f32[4,8,128]{2,1,0:T(8,128)S(1)}, f32[4,8,128]{2,1,0:T(8,128)}, u32[]{:S(2)}) copy-start(f32[4,8,128]{2,1,0:T(8,128)} %band_ref.1) | copy-start | bytes 49156
  28.0 4.3 %copy-start.1 = (f32[4,8,128]{2,1,0:T(8,128)S(1)}, f32[4,8,128]{2,1,0:T(8,128)}, u32[]{:S(2)}) copy-start(f32[4,8,128]{2,1,0:T(8,128)} %res_ref.1) | copy-start | bytes 49156
  48.9 19.4 %copy-start.2 = (f32[4,8,128]{2,1,0:T(8,128)S(1)}, f32[4,8,128]{2,1,0:T(8,128)}, u32[]{:S(2)}) copy-start(f32[4,8,128]{2,1,0:T(8,128)} %iter_ref.1) | copy-start | bytes 49156

commit v5 on v4

--- a/solution.py
+++ b/solution.py
@@ -31,8 +31,12 @@
     return jax.ShapeDtypeStruct(dims, dtype)
 
 
+def base_index():
+    return lax.axis_index("y") * lax.axis_size("x") + lax.axis_index("x")
+
+
 def group_place(blocks):
-    block = lax.axis_index("base")
+    block = base_index()
     first = jnp.where(block % 2 == 1, block, (block + blocks - 1) % blocks)
     return 1 - block % 2 + 2 * jnp.where(first >= blocks // 2, 1, 0)
 
@@ -67,7 +71,7 @@
     slots = 4 * owned
     slot = lax.broadcasted_iota(jnp.int32, (slots, 2 * rows), 0)
     kind = slot // owned
-    block = lax.axis_index("base")
+    block = base_index()
     turn_up = 1 - 2 * (block % 2)
     offset = jnp.where(kind == 0, 0, jnp.where(kind == 1, turn_up, jnp.where(kind == 2, -turn_up, blocks // 2)))
     station = ((block + offset + blocks) % blocks) * owned + slot % owned
@@ -203,7 +207,7 @@
     place = group_place(blocks)
     odd_place = place + 1 - 2 * (place % 2)
     far_place = (place + 2) % 4
-    partner = even_ref.at[1 - lax.axis_index("base") % 2]
+    partner = even_ref.at[1 - base_index() % 2]
     sources = (own_ref, partner, odd_ref, far_ref)
     for k, ref in enumerate(sources):
         for j in range(16):
@@ -294,7 +298,7 @@
     freq = frequencies(chan_index(), width, channels)
     cosine = turn_ref[0:half, :]
     sine = turn_ref[half : 2 * half, :]
-    total = even_ref[1 - lax.axis_index("base") % 2]
+    total = even_ref[1 - base_index() % 2]
     for k in range(4):
         total = total + group_ref[k]
     moved = jnp.zeros((half, width), f32)
@@ -332,16 +336,29 @@
     row_ref[...] = jnp.broadcast_to(row, row_ref.shape)
 
 
+def line_kernel(rows_ref, out_ref, *, across):
+    count, width = rows_ref.shape
+    lines, part = count // across, width // across
+    lane = lax.broadcasted_iota(jnp.int32, (1, width), 1)
+    total = jnp.zeros((1, width), f32)
+    for x in range(across):
+        line = jnp.sum(rows_ref[x * lines : (x + 1) * lines, :], axis=0, keepdims=True)
+        line = jnp.where(lane < part, line, 0.0)
+        total = total + (pltpu.roll(line, x * part, 1) if x else line)
+    out_ref[...] = jnp.broadcast_to(total, out_ref.shape)
+
+
 def update_kernel(
     rows_ref, curv_ref, small_ref, band_ref, res_ref, iter_ref,
-    iter_out, iter_delay_out, res_out, res_delay_out, dir_out, dir_delay_out
+    iter_out, iter_delay_out, res_out, res_delay_out, dir_out, dir_delay_out, *, across
 ):
     rows = rows_ref[...]
     count, width = rows.shape
     owned = band_ref.shape[0]
     half = 2 * owned
     sums = jnp.sum(rows, axis=0, keepdims=True)
-    lane = lax.broadcasted_iota(jnp.int32, (1, width), 1)
+    part = width // across
+    lane = lax.broadcasted_iota(jnp.int32, (1, width), 1) % part
 
     def scalar(x):
         return jnp.sum(x, axis=1, keepdims=True)
@@ -351,7 +368,7 @@
     lefts = pltpu.roll(rows, width - 24, 1)
     curves = pair + damping_weight * moves
     valid = (lax.broadcasted_iota(jnp.int32, (count, width), 0) % 2 == 0) & (
-        lax.broadcasted_iota(jnp.int32, (count, width), 1) < half
+        lax.broadcasted_iota(jnp.int32, (count, width), 1) % part < half
     )
 
     def delays(x):
@@ -373,8 +390,11 @@
     res_out[...] = new_res
     dir_out[...] = new_res + ratio3 * band
 
-    mine = lax.broadcasted_iota(jnp.int32, (count, width), 0) == 2 * lax.axis_index("base")
-    own = jnp.sum(jnp.where(mine, pair, 0.0), axis=0, keepdims=True)
+    mine = lax.broadcasted_iota(jnp.int32, (count, width), 0) == 2 * lax.axis_index("y")
+    line = jnp.sum(jnp.where(mine, pair, 0.0), axis=0, keepdims=True)
+    own = jnp.zeros((1, half), f32)
+    for x in range(across):
+        own = own + jnp.where(lax.axis_index("x") == x, line[:, x * part : x * part + half], 0.0)
     own = jnp.concatenate([own[:, 0:owned], own[:, owned:half]], axis=0)
     move = small_ref[0]
     iter_delay_out[...] = small_ref[2] + alpha * move
@@ -398,9 +418,10 @@
 ):
     owned, _, width = gains.shape
     rows = model.shape[0]
-    blocks = lax.axis_size("base")
-    lines = lax.axis_size("z")
-    cores = lax.axis_size("core")
+    rings, lines = lax.axis_size("y"), lax.axis_size("z")
+    across, cores = lax.axis_size("x"), lax.axis_size("core")
+    blocks = rings * across
+    base = ("y", "x")
     channels = width * lines * cores
     slots = 4 * owned
     factor = owned / (2.0 * rows)
@@ -447,16 +468,16 @@
     def exchange(to_even, to_group):
         count = to_group.shape[1]
         group = lax.all_to_all(
-            to_group.reshape(4 * count, width), "base", 0, 0, axis_index_groups=groups, tiled=True
+            to_group.reshape(4 * count, width), base, 0, 0, axis_index_groups=groups, tiled=True
         )
-        even = lax.all_gather(to_even, "base", axis_index_groups=even_groups)
+        even = lax.all_gather(to_even, base, axis_index_groups=even_groups)
         return even, group.reshape(4, count, width)
 
     far_pairs = [(i, (i + half) % blocks) for i in range(blocks)]
     odd_pairs = [(i, (i + 1) % blocks if i % 2 else (i - 1) % blocks) for i in range(blocks)]
-    from_far = lax.ppermute(terms, "base", far_pairs)
-    from_odd = lax.ppermute(terms, "base", odd_pairs)
-    from_even = lax.all_gather(terms, "base", axis_index_groups=even_groups)
+    from_far = lax.ppermute(terms, base, far_pairs)
+    from_odd = lax.ppermute(terms, base, odd_pairs)
+    from_even = lax.all_gather(terms, base, axis_index_groups=even_groups)
 
     to_even, to_group = pl.pallas_call(
         lambda *refs: baseline_kernel(*refs, factor=factor, blocks=blocks),
@@ -475,20 +496,26 @@
 
     curv, row = pl.pallas_call(
         lambda *refs: curvature_kernel(*refs, channels=channels),
-        out_shape=(shape(owned, 8, width), shape(lines, width)),
+        out_shape=(shape(owned, 8, width), shape(across * lines, width)),
         in_specs=[vmem()] * 7,
         out_specs=(vmem(), vmem()),
         compiler_params=params(4),
         name="curvature",
     )(*exchange(to_even, to_group), terms, turn, small, dir_band, res_band)
 
-    line = lax.all_to_all(row, "z", 0, 0, tiled=True)
-    peers = blocks * cores
-    line = jnp.broadcast_to(jnp.sum(line, axis=0, keepdims=True), (peers, width))
-    everyone = lax.all_to_all(line, ("base", "core"), 0, 0, tiled=True)
+    row = lax.all_to_all(row, ("x", "z"), 0, 0, tiled=True)
+    row = pl.pallas_call(
+        lambda *refs: line_kernel(*refs, across=across),
+        out_shape=shape(rings * cores, width),
+        in_specs=[vmem()],
+        out_specs=vmem(),
+        compiler_params=params(4),
+        name="line_sums",
+    )(row)
+    everyone = lax.all_to_all(row, ("y", "core"), 0, 0, tiled=True)
 
     outs = pl.pallas_call(
-        update_kernel,
+        lambda *refs: update_kernel(*refs, across=across),
         out_shape=(
             shape(owned, 8, width),
             shape(2, owned),
@@ -513,12 +540,15 @@
 
 
 def solution(mesh):
-    cores = 2
+    cores, across = 2, 4
     blocks, chans = mesh.shape["base"], mesh.shape["chan"]
-    split = Mesh(mesh.devices.reshape(blocks, chans // cores, cores), ("base", "z", "core"))
-    band = P("base", None, ("z", "core"))
-    delay = P("base", None)
-    one = P("base")
+    split = Mesh(
+        mesh.devices.reshape(blocks // across, across, chans // cores, cores), ("y", "x", "z", "core")
+    )
+    base, chan = ("y", "x"), ("z", "core")
+    band = P(base, None, chan)
+    delay = P(base, None)
+    one = P(base)
     return jax.shard_map(
         body,
         mesh=split,

time: 69.5 us -> 69.3 us (level)
  no operation moved by 1% of the time
where the time goes in v5:
time: 69.3 us; the launch traced here: 68.8 us
  blocking collectives  42.5 us (61%)
  starting transfers between devices  19.3 us (28%)
  Pallas kernels  5.44 us (8%)
  waiting for transfers between devices  0.96 us (1%)
    all_to_all x1, blocking collectives, body(): row = lax.all_to_all(row, ('x', 'z'), 0, 0, tiled=True)  20.4 us
    all_to_all x1, blocking collectives, body(): everyone = lax.all_to_all(row, ('y', 'core'), 0, 0, tiled=True)  15.1 us
    ppermute x1, starting transfers between devices, body(): from_far = lax.ppermute(terms, base, far_pairs)  8.28 us
    all_to_all x1, starting transfers between devices, exchange(): lax.all_to_all(to_group.reshape(4 * count, width), base, 0, 0, axis_index...  6.73 us
    ppermute x1, starting transfers between devices, body(): from_odd = lax.ppermute(terms, base, odd_pairs)  4.27 us
    all_gather x1, blocking collectives, body(): from_even = lax.all_gather(terms, base, axis_index_groups=even_groups)  3.63 us
    all_gather x1, blocking collectives, exchange(): even = lax.all_gather(to_even, base, axis_index_groups=even_groups)  3.38 us
    pallas_call x1, Pallas kernels, body(): pl.pallas_call(lambda *refs: baseline_kernel(*refs, factor=factor, blocks...  3.14 us
  transfers between devices with their start and end apart: 3, of which 2 were waited for; matrix products, arithmetic and copies ran while one was open for 0% of the time, Pallas kernels for 0%

profile of v5, /device:TPU:1, one launch (start us, length us, event | category | flops | bytes accessed | tf_op | source)
XLA Modules:
  0.0 68.8 jit_solution(12727468122391068598)
XLA Ops:
  0.6 1.2 %station_terms.1 = (f32[64,128]{1,0:T(8,128)S(1)}, f32[16,128]{1,0:T(8,128)S(1)}, f32[3,2,4]{2,1,0:T(2,128)S(1)}, bf16[512,128]{1,0:T(8,128)(2,1)S(1)}, bf16[16,...) custom-call(f32[4,8,128]{2,1,0:T(8,128)} %refs_0_.1, f32[4,8,128]{2,1,0:T(8,128)} %refs_3_.1, f32[2,4]{1,0:T(2,128)} %bitcast.27, ...), custom_call_target="tpu_custom_call" | custom-call | tf_op jit(solution)/shard_map/station_terms/pallas_call | solution.py:432
  1.9 8.3 %collective-permute-start.1 = (f32[64,128]{1,0:T(8,128)S(1)}, f32[64,128]{1,0:T(8,128)S(1)}, u32[]{:S(2)}, u32[]{:S(2)}) collective-permute-start(f32[64,128]{1,0:T(8,128)S(1)} %get-tuple-element.22.refs_0_.refs_2_), channel_id=1, source_target_pairs={{0,256},{16,272},{32,288},{48,304},{64,320},{80,336},{96,352},{112... | collective-permute-start | bytes 98312 | tf_op jit(solution)/shard_map/ppermute | solution.py:478
  10.2 4.3 %collective-permute-start = (f32[64,128]{1,0:T(8,128)S(1)}, f32[64,128]{1,0:T(8,128)S(1)}, u32[]{:S(2)}, u32[]{:S(2)}) collective-permute-start(f32[64,128]{1,0:T(8,128)S(1)} %get-tuple-element.22.refs_0_.refs_2_), channel_id=1, source_target_pairs={{0,496},{16,32},{32,16},{48,64},{64,48},{80,96},{96,80},{112,128},... | collective-permute-start | bytes 98312 | tf_op jit(solution)/shard_map/ppermute | solution.py:479
  14.4 3.6 %all-gather = f32[128,128]{1,0:T(8,128)S(1)} all-gather(f32[64,128]{1,0:T(8,128)S(1)} %get-tuple-element.22.refs_0_.refs_2_), channel_id=2, replica_groups={{0,16},{32,48},{64,80},{96,112},{128,144},{160,176},{192,208},{224,240}..., dimensions={0}, use_global_device_ids=true | all-gather | bytes 98304 | tf_op jit(solution)/shard_map/all_gather | solution.py:480
  18.1 0.0 collective-permute-done.1.refs_3_
  18.1 0.1 collective-permute-done.refs_2_
  18.1 3.1 %baselines.1 = (f32[32,128]{1,0:T(8,128)S(1)}, f32[4,32,128]{2,1,0:T(8,128)}) custom-call(f32[64,128]{1,0:T(8,128)S(1)} %get-tuple-element.22.refs_0_.refs_2_, f32[2,64,128]{2,1,0:T(8,128)S(1)} %bitcast.20, f32[64,128]{1,0:T(8,128)S(1)} %collective-permute-done.refs_2_, f32[64,128]{1,0:T(8,128)S(1)} %collective-permute-done.1.refs_3_, ...), custom_call_target="tpu_custom_call" | custom-call | tf_op jit(solution)/shard_map/baselines/pallas_call | solution.py:482
  21.3 6.7 %all-to-all-start = ((f32[4,32,128]{2,1,0:T(8,128)}), f32[4,32,128]{2,1,0:T(8,128)S(1)}, u32[]{:S(2)}, u32[]{:S(2)}) async-start(f32[4,32,128]{2,1,0:T(8,128)} %get-tuple-element.27), calls=%async_computation | async-start | bytes 131072 | tf_op jit(solution)/shard_map/all_to_all | solution.py:470
  28.0 0.0 copy-start
  28.0 0.0 copy-start.1
  28.0 3.4 %all-gather.1 = f32[64,128]{1,0:T(8,128)S(1)} all-gather(f32[32,128]{1,0:T(8,128)S(1)} %get-tuple-element.26), channel_id=3, replica_groups={{0,16},{32,48},{64,80},{96,112},{128,144},{160,176},{192,208},{224,240}..., dimensions={0}, use_global_device_ids=true | all-gather | bytes 49152 | tf_op jit(solution)/shard_map/all_gather | solution.py:473
  31.4 0.9 %all-to-all-done.refs_1_ = f32[4,32,128]{2,1,0:T(8,128)S(1)} async-done(((f32[4,32,128]{2,1,0:T(8,128)}), f32[4,32,128]{2,1,0:T(8,128)S(1)}, u32[]{:S(2)}, u32[]{:S(2)}) %all-to-all-start) | async-done | bytes 65568 | tf_op jit(solution)/shard_map/all_to_all | solution.py:470
  32.3 0.0 copy-done
  32.3 0.0 copy-done.1
  32.3 0.2 curvature.1
  32.5 20.4 %all_to_all.28 = f32[32,1,128]{2,1,0:T(1,128)S(1)} all-to-all(f32[32,1,128]{2,1,0:T(1,128)S(1)} %bitcast.25), channel_id=1, replica_groups=mesh['y'=8,'x'=4,'z'=8,'core'=2] {'x','z'}, dimensions={0} | all-to-all | bytes 32768 | tf_op jit(solution)/shard_map/all_to_all | solution.py:506
  52.9 0.1 line_sums.1
  53.0 0.0 copy-start.2
  53.0 15.1 %all_to_all.29 = f32[16,1,128]{2,1,0:T(1,128)S(1)} all-to-all(f32[16,1,128]{2,1,0:T(1,128)S(1)} %bitcast.24), channel_id=1, replica_groups=mesh['y'=8,'x'=4,'z'=8,'core'=2] {'y','core'}, dimensions={0} | all-to-all | bytes 16384 | tf_op jit(solution)/shard_map/all_to_all | solution.py:515
  68.0 0.0 copy-done.2
  68.0 0.8 %update.1 = (f32[4,8,128]{2,1,0:T(8,128)}, f32[2,4]{1,0:T(2,128)}, f32[4,8,128]{2,1,0:T(8,128)}, f32[2,4]{1,0:T(2,128)}, f32[4,8,128]{2,1,0:T(8,128)}, /*index=5*/f32[2,4]{1,0:T(2,128)}) custom-call(f32[16,128]{1,0:T(8,128)S(1)} %bitcast.23, f32[4,8,128]{2,1,0:T(8,128)S(1)} %get-tuple-element.31.refs_1_, f32[3,2,4]{2,1,0:T(2,128)S(1)} %get-tuple-element.29.refs_4_.refs_2_, ...), custom_call_target="tpu_custom_call" | custom-call | tf_op jit(solution)/shard_map/update/pallas_call | solution.py:517
Async XLA Ops:
  1.9 16.2 %collective-permute-start.1 = (f32[64,128]{1,0:T(8,128)S(1)}, f32[64,128]{1,0:T(8,128)S(1)}, u32[]{:S(2)}, u32[]{:S(2)}) collective-permute-start(f32[64,128]{1,0:T(8,128)S(1)} %get-tuple-element.22.refs_0_.refs_2_), channel_id=1, source_target_pairs={{0,256},{16,272},{32,288},{48,304},{64,320},{80,336},{96,352},{112... | collective-permute-start | bytes 98312 | tf_op jit(solution)/shard_map/ppermute | solution.py:478
  10.2 8.0 %collective-permute-start = (f32[64,128]{1,0:T(8,128)S(1)}, f32[64,128]{1,0:T(8,128)S(1)}, u32[]{:S(2)}, u32[]{:S(2)}) collective-permute-start(f32[64,128]{1,0:T(8,128)S(1)} %get-tuple-element.22.refs_0_.refs_2_), channel_id=1, source_target_pairs={{0,496},{16,32},{32,16},{48,64},{64,48},{80,96},{96,80},{112,128},... | collective-permute-start | bytes 98312 | tf_op jit(solution)/shard_map/ppermute | solution.py:479
  21.3 11.0 %all-to-all-start = ((f32[4,32,128]{2,1,0:T(8,128)}), f32[4,32,128]{2,1,0:T(8,128)S(1)}, u32[]{:S(2)}, u32[]{:S(2)}) async-start(f32[4,32,128]{2,1,0:T(8,128)} %get-tuple-element.27), calls=%async_computation | async-start | bytes 131072 | tf_op jit(solution)/shard_map/all_to_all | solution.py:470
  28.0 4.3 %copy-start = (f32[4,8,128]{2,1,0:T(8,128)S(1)}, f32[4,8,128]{2,1,0:T(8,128)}, u32[]{:S(2)}) copy-start(f32[4,8,128]{2,1,0:T(8,128)} %refs_3_.1) | copy-start | bytes 49156
  28.0 4.3 %copy-start.1 = (f32[4,8,128]{2,1,0:T(8,128)S(1)}, f32[4,8,128]{2,1,0:T(8,128)}, u32[]{:S(2)}) copy-start(f32[4,8,128]{2,1,0:T(8,128)} %refs_4_.1) | copy-start | bytes 49156
  53.0 15.1 %copy-start.2 = (f32[4,8,128]{2,1,0:T(8,128)S(1)}, f32[4,8,128]{2,1,0:T(8,128)}, u32[]{:S(2)}) copy-start(f32[4,8,128]{2,1,0:T(8,128)} %refs_5_.3) | copy-start | bytes 49156

commit v6 on v5

--- a/solution.py
+++ b/solution.py
@@ -197,7 +197,7 @@
 
 def baseline_kernel(
     own_ref, even_ref, odd_ref, far_ref, model_ref, gather_ref, scatter_ref,
-    even_out, group_out, table, picked, grads, model_parts, *, factor, blocks
+    even_out, group_hbm, table, picked, grads, model_parts, group_out, sems, *, factor, blocks
 ):
     _, rows, width = model_parts.shape
     slots = table.shape[0]
@@ -255,7 +255,7 @@
         for c, value in zip(cols, adjoint_times(change, left)):
             grads[at_q, c] = value
 
-    def collect(first):
+    def collect(first, then):
         for n in range(0, 8 * width, step):
             total = None
             for base in (first, rows + first):
@@ -271,6 +271,26 @@
                 table[:, n : n + step] = table[:, n : n + step] + factor * total
             else:
                 table[:, n : n + step] = factor * total
+            if then is not None:
+                then(n)
+
+    group_out[(odd_place + 2) % 4] = jnp.zeros(even_out.shape, f32)
+    sinks = (group_out.at[place], even_out, group_out.at[odd_place], group_out.at[far_place])
+    copies = []
+
+    def deliver(n):
+        first = n // width
+        for k, ref in enumerate(sinks):
+            for j in (first, first + 1):
+                ref[j * owned : (j + 1) * owned, :] = table[
+                    k * owned : (k + 1) * owned, j * width : (j + 1) * width
+                ]
+        at = pl.ds(first * owned, 2 * owned)
+        copy = pltpu.make_async_copy(
+            group_out.at[:, at, :], group_hbm.at[:, at, :], sems.at[n // step]
+        )
+        copy.start()
+        copies.append(copy)
 
     load(0)
     for first in range(0, rows, stage):
@@ -278,14 +298,10 @@
             load(first + stage)
         for i in range(first // 8, (first + stage) // 8):
             chunk(i)
-        collect(first)
-    group_out[(odd_place + 2) % 4] = jnp.zeros(even_out.shape, f32)
-    sinks = (group_out.at[place], even_out, group_out.at[odd_place], group_out.at[far_place])
-    for k, ref in enumerate(sinks):
-        for j in range(8):
-            ref[j * owned : (j + 1) * owned, :] = table[
-                k * owned : (k + 1) * owned, j * width : (j + 1) * width
-            ]
+        last = first + stage == rows
+        collect(first, deliver if last else None)
+    for copy in copies:
+        copy.wait()
 
 
 def curvature_kernel(
@@ -483,12 +499,14 @@
         lambda *refs: baseline_kernel(*refs, factor=factor, blocks=blocks),
         out_shape=(shape(8 * owned, width), shape(4, 8 * owned, width)),
         in_specs=[vmem()] * 7,
-        out_specs=(vmem(),) * 2,
+        out_specs=(vmem(), hbm()),
         scratch_shapes=[
             pltpu.VMEM((slots, 16 * width), f32),
             pltpu.VMEM((2 * rows, 16 * width), f32),
             pltpu.VMEM((2 * rows, 8 * width), f32),
             pltpu.VMEM((8, rows, width), f32),
+            pltpu.VMEM((4, 8 * owned, width), f32),
+            pltpu.SemaphoreType.DMA((4,)),
         ],
         compiler_params=params(24),
         name="baselines",

time: 69.3 us -> 69.3 us (level)
  no operation moved by 1% of the time
where the time goes in v6:
time: 69.3 us; the launch traced here: 68.9 us
  blocking collectives  42.5 us (61%)
  starting transfers between devices  19.3 us (28%)
  Pallas kernels  5.47 us (8%)
  waiting for transfers between devices  0.96 us (1%)
    all_to_all x1, blocking collectives, body(): row = lax.all_to_all(row, ('x', 'z'), 0, 0, tiled=True)  20.4 us
    all_to_all x1, blocking collectives, body(): everyone = lax.all_to_all(row, ('y', 'core'), 0, 0, tiled=True)  15.1 us
    ppermute x1, starting transfers between devices, body(): from_far = lax.ppermute(terms, base, far_pairs)  8.28 us
    all_to_all x1, starting transfers between devices, exchange(): lax.all_to_all(to_group.reshape(4 * count, width), base, 0, 0, axis_index...  6.73 us
    ppermute x1, starting transfers between devices, body(): from_odd = lax.ppermute(terms, base, odd_pairs)  4.27 us
    all_gather x1, blocking collectives, body(): from_even = lax.all_gather(terms, base, axis_index_groups=even_groups)  3.63 us
    all_gather x1, blocking collectives, exchange(): even = lax.all_gather(to_even, base, axis_index_groups=even_groups)  3.38 us
    pallas_call x1, Pallas kernels, body(): pl.pallas_call(lambda *refs: baseline_kernel(*refs, factor=factor, blocks...  3.17 us
  transfers between devices with their start and end apart: 3, of which 2 were waited for; matrix products, arithmetic and copies ran while one was open for 0% of the time, Pallas kernels for 0%

profile of v6, /device:TPU:1, one launch (start us, length us, event | category | flops | bytes accessed | tf_op | source)
XLA Modules:
  0.0 68.9 jit_solution(5363062522283708382)
XLA Ops:
  0.6 1.2 %station_terms.1 = (f32[64,128]{1,0:T(8,128)S(1)}, f32[16,128]{1,0:T(8,128)S(1)}, f32[3,2,4]{2,1,0:T(2,128)S(1)}, bf16[512,128]{1,0:T(8,128)(2,1)S(1)}, bf16[16,...) custom-call(f32[4,8,128]{2,1,0:T(8,128)} %refs_0_.1, f32[4,8,128]{2,1,0:T(8,128)} %refs_3_.1, f32[2,4]{1,0:T(2,128)} %bitcast.27, ...), custom_call_target="tpu_custom_call" | custom-call | tf_op jit(solution)/shard_map/station_terms/pallas_call | solution.py:448
  1.9 8.3 %collective-permute-start.1 = (f32[64,128]{1,0:T(8,128)S(1)}, f32[64,128]{1,0:T(8,128)S(1)}, u32[]{:S(2)}, u32[]{:S(2)}) collective-permute-start(f32[64,128]{1,0:T(8,128)S(1)} %get-tuple-element.22.refs_0_.refs_2_), channel_id=1, source_target_pairs={{0,256},{16,272},{32,288},{48,304},{64,320},{80,336},{96,352},{112... | collective-permute-start | bytes 98312 | tf_op jit(solution)/shard_map/ppermute | solution.py:494
  10.2 4.3 %collective-permute-start = (f32[64,128]{1,0:T(8,128)S(1)}, f32[64,128]{1,0:T(8,128)S(1)}, u32[]{:S(2)}, u32[]{:S(2)}) collective-permute-start(f32[64,128]{1,0:T(8,128)S(1)} %get-tuple-element.22.refs_0_.refs_2_), channel_id=1, source_target_pairs={{0,496},{16,32},{32,16},{48,64},{64,48},{80,96},{96,80},{112,128},... | collective-permute-start | bytes 98312 | tf_op jit(solution)/shard_map/ppermute | solution.py:495
  14.4 3.6 %all-gather = f32[128,128]{1,0:T(8,128)S(1)} all-gather(f32[64,128]{1,0:T(8,128)S(1)} %get-tuple-element.22.refs_0_.refs_2_), channel_id=2, replica_groups={{0,16},{32,48},{64,80},{96,112},{128,144},{160,176},{192,208},{224,240}..., dimensions={0}, use_global_device_ids=true | all-gather | bytes 98304 | tf_op jit(solution)/shard_map/all_gather | solution.py:496
  18.1 0.0 collective-permute-done.1.refs_3_
  18.1 0.1 collective-permute-done.refs_2_
  18.1 3.2 %baselines.1 = (f32[32,128]{1,0:T(8,128)S(1)}, f32[4,32,128]{2,1,0:T(8,128)}) custom-call(f32[64,128]{1,0:T(8,128)S(1)} %get-tuple-element.22.refs_0_.refs_2_, f32[2,64,128]{2,1,0:T(8,128)S(1)} %bitcast.20, f32[64,128]{1,0:T(8,128)S(1)} %collective-permute-done.refs_2_, f32[64,128]{1,0:T(8,128)S(1)} %collective-permute-done.1.refs_3_, ...), custom_call_target="tpu_custom_call" | custom-call | tf_op jit(solution)/shard_map/baselines/pallas_call | solution.py:498
  21.3 6.7 %all-to-all-start = ((f32[4,32,128]{2,1,0:T(8,128)}), f32[4,32,128]{2,1,0:T(8,128)S(1)}, u32[]{:S(2)}, u32[]{:S(2)}) async-start(f32[4,32,128]{2,1,0:T(8,128)} %get-tuple-element.27), calls=%async_computation | async-start | bytes 131072 | tf_op jit(solution)/shard_map/all_to_all | solution.py:486
  28.1 0.0 copy-start
  28.1 0.0 copy-start.1
  28.1 3.4 %all-gather.1 = f32[64,128]{1,0:T(8,128)S(1)} all-gather(f32[32,128]{1,0:T(8,128)S(1)} %get-tuple-element.26), channel_id=3, replica_groups={{0,16},{32,48},{64,80},{96,112},{128,144},{160,176},{192,208},{224,240}..., dimensions={0}, use_global_device_ids=true | all-gather | bytes 49152 | tf_op jit(solution)/shard_map/all_gather | solution.py:489
  31.4 0.9 %all-to-all-done.refs_1_ = f32[4,32,128]{2,1,0:T(8,128)S(1)} async-done(((f32[4,32,128]{2,1,0:T(8,128)}), f32[4,32,128]{2,1,0:T(8,128)S(1)}, u32[]{:S(2)}, u32[]{:S(2)}) %all-to-all-start) | async-done | bytes 65568 | tf_op jit(solution)/shard_map/all_to_all | solution.py:486
  32.3 0.0 copy-done
  32.3 0.0 copy-done.1
  32.3 0.2 curvature.1
  32.6 20.4 %all_to_all.28 = f32[32,1,128]{2,1,0:T(1,128)S(1)} all-to-all(f32[32,1,128]{2,1,0:T(1,128)S(1)} %bitcast.25), channel_id=1, replica_groups=mesh['y'=8,'x'=4,'z'=8,'core'=2] {'x','z'}, dimensions={0} | all-to-all | bytes 32768 | tf_op jit(solution)/shard_map/all_to_all | solution.py:524
  52.9 0.1 line_sums.1
  53.0 0.0 copy-start.2
  53.0 15.1 %all_to_all.29 = f32[16,1,128]{2,1,0:T(1,128)S(1)} all-to-all(f32[16,1,128]{2,1,0:T(1,128)S(1)} %bitcast.24), channel_id=1, replica_groups=mesh['y'=8,'x'=4,'z'=8,'core'=2] {'y','core'}, dimensions={0} | all-to-all | bytes 16384 | tf_op jit(solution)/shard_map/all_to_all | solution.py:533
  68.1 0.0 copy-done.2
  68.1 0.8 %update.1 = (f32[4,8,128]{2,1,0:T(8,128)}, f32[2,4]{1,0:T(2,128)}, f32[4,8,128]{2,1,0:T(8,128)}, f32[2,4]{1,0:T(2,128)}, f32[4,8,128]{2,1,0:T(8,128)}, /*index=5*/f32[2,4]{1,0:T(2,128)}) custom-call(f32[16,128]{1,0:T(8,128)S(1)} %bitcast.23, f32[4,8,128]{2,1,0:T(8,128)S(1)} %get-tuple-element.31.refs_1_, f32[3,2,4]{2,1,0:T(2,128)S(1)} %get-tuple-element.29.refs_4_.refs_2_, ...), custom_call_target="tpu_custom_call" | custom-call | tf_op jit(solution)/shard_map/update/pallas_call | solution.py:535
Async XLA Ops:
  1.9 16.2 %collective-permute-start.1 = (f32[64,128]{1,0:T(8,128)S(1)}, f32[64,128]{1,0:T(8,128)S(1)}, u32[]{:S(2)}, u32[]{:S(2)}) collective-permute-start(f32[64,128]{1,0:T(8,128)S(1)} %get-tuple-element.22.refs_0_.refs_2_), channel_id=1, source_target_pairs={{0,256},{16,272},{32,288},{48,304},{64,320},{80,336},{96,352},{112... | collective-permute-start | bytes 98312 | tf_op jit(solution)/shard_map/ppermute | solution.py:494
  10.2 8.0 %collective-permute-start = (f32[64,128]{1,0:T(8,128)S(1)}, f32[64,128]{1,0:T(8,128)S(1)}, u32[]{:S(2)}, u32[]{:S(2)}) collective-permute-start(f32[64,128]{1,0:T(8,128)S(1)} %get-tuple-element.22.refs_0_.refs_2_), channel_id=1, source_target_pairs={{0,496},{16,32},{32,16},{48,64},{64,48},{80,96},{96,80},{112,128},... | collective-permute-start | bytes 98312 | tf_op jit(solution)/shard_map/ppermute | solution.py:495
  21.3 11.0 %all-to-all-start = ((f32[4,32,128]{2,1,0:T(8,128)}), f32[4,32,128]{2,1,0:T(8,128)S(1)}, u32[]{:S(2)}, u32[]{:S(2)}) async-start(f32[4,32,128]{2,1,0:T(8,128)} %get-tuple-element.27), calls=%async_computation | async-start | bytes 131072 | tf_op jit(solution)/shard_map/all_to_all | solution.py:486
  28.1 4.3 %copy-start = (f32[4,8,128]{2,1,0:T(8,128)S(1)}, f32[4,8,128]{2,1,0:T(8,128)}, u32[]{:S(2)}) copy-start(f32[4,8,128]{2,1,0:T(8,128)} %refs_3_.1) | copy-start | bytes 49156
  28.1 4.3 %copy-start.1 = (f32[4,8,128]{2,1,0:T(8,128)S(1)}, f32[4,8,128]{2,1,0:T(8,128)}, u32[]{:S(2)}) copy-start(f32[4,8,128]{2,1,0:T(8,128)} %refs_4_.1) | copy-start | bytes 49156
  53.0 15.1 %copy-start.2 = (f32[4,8,128]{2,1,0:T(8,128)S(1)}, f32[4,8,128]{2,1,0:T(8,128)}, u32[]{:S(2)}) copy-start(f32[4,8,128]{2,1,0:T(8,128)} %refs_5_.3) | copy-start | bytes 49156

commit v7 on v5

--- a/solution.py
+++ b/solution.py
@@ -230,12 +230,16 @@
     cols = [slice(j * width, (j + 1) * width) for j in range(16)]
     stage = rows // 2
     def load(first):
-        for g in range(first // group, (first + stage) // group):
-            part = jnp.dot(
-                shuffle, model_ref[g * size : (g + 1) * size, :], preferred_element_type=f32
-            )
+        for g in range(first // group, (first + stage) // group, 2):
+            both = jnp.concatenate(
+                [model_ref[k * size : (k + 1) * size, :] for k in (g, g + 1)], axis=1
+            )
+            part = jnp.dot(shuffle, both, preferred_element_type=f32)
             for j in range(8):
-                model_parts[j, g * group : (g + 1) * group, :] = part[j * group : (j + 1) * group, :]
+                for k in range(2):
+                    model_parts[j, (g + k) * group : (g + k + 1) * group, :] = part[
+                        j * group : (j + 1) * group, k * width : (k + 1) * width
+                    ]
         for base in (first, rows + first):
             pick = gather_ref[base : base + stage, :]
             for n in range(0, 16 * width, step):
@@ -263,8 +267,10 @@
                 sel = scatter_ref[:, base : base + stage]
                 high = value.astype(bf16)
                 low = (value - high.astype(f32)).astype(bf16)
-                part = jnp.dot(sel, high, preferred_element_type=f32) + jnp.dot(
-                    sel, low, preferred_element_type=f32
+                part = jnp.dot(
+                    jnp.concatenate([sel, sel], axis=1),
+                    jnp.concatenate([high, low], axis=0),
+                    preferred_element_type=f32,
                 )
                 total = part if total is None else total + part
             if first:

time: 69.3 us -> 69.2 us (level)
  no operation moved by 1% of the time
where the time goes in v7:
time: 69.2 us; the launch traced here: 68.7 us
  blocking collectives  42.5 us (61%)
  starting transfers between devices  19.3 us (28%)
  Pallas kernels  5.34 us (8%)
  waiting for transfers between devices  0.95 us (1%)
    all_to_all x1, blocking collectives, body(): row = lax.all_to_all(row, ('x', 'z'), 0, 0, tiled=True)  20.4 us
    all_to_all x1, blocking collectives, body(): everyone = lax.all_to_all(row, ('y', 'core'), 0, 0, tiled=True)  15.1 us
    ppermute x1, starting transfers between devices, body(): from_far = lax.ppermute(terms, base, far_pairs)  8.28 us
    all_to_all x1, starting transfers between devices, exchange(): lax.all_to_all(to_group.reshape(4 * count, width), base, 0, 0, axis_index...  6.72 us
    ppermute x1, starting transfers between devices, body(): from_odd = lax.ppermute(terms, base, odd_pairs)  4.27 us
    all_gather x1, blocking collectives, body(): from_even = lax.all_gather(terms, base, axis_index_groups=even_groups)  3.63 us
    all_gather x1, blocking collectives, exchange(): even = lax.all_gather(to_even, base, axis_index_groups=even_groups)  3.38 us
    pallas_call x1, Pallas kernels, body(): pl.pallas_call(lambda *refs: baseline_kernel(*refs, factor=factor, blocks...  3.05 us
  transfers between devices with their start and end apart: 3, of which 2 were waited for; matrix products, arithmetic and copies ran while one was open for 0% of the time, Pallas kernels for 0%

profile of v7, /device:TPU:1, one launch (start us, length us, event | category | flops | bytes accessed | tf_op | source)
XLA Modules:
  0.0 68.7 jit_solution(1450768225098632692)
XLA Ops:
  0.6 1.2 %station_terms.1 = (f32[64,128]{1,0:T(8,128)S(1)}, f32[16,128]{1,0:T(8,128)S(1)}, f32[3,2,4]{2,1,0:T(2,128)S(1)}, bf16[512,128]{1,0:T(8,128)(2,1)S(1)}, bf16[16,...) custom-call(f32[4,8,128]{2,1,0:T(8,128)} %refs_0_.1, f32[4,8,128]{2,1,0:T(8,128)} %refs_3_.1, f32[2,4]{1,0:T(2,128)} %bitcast.27, ...), custom_call_target="tpu_custom_call" | custom-call | tf_op jit(solution)/shard_map/station_terms/pallas_call | solution.py:438
  1.9 8.3 %collective-permute-start.1 = (f32[64,128]{1,0:T(8,128)S(1)}, f32[64,128]{1,0:T(8,128)S(1)}, u32[]{:S(2)}, u32[]{:S(2)}) collective-permute-start(f32[64,128]{1,0:T(8,128)S(1)} %get-tuple-element.22.refs_0_.refs_2_), channel_id=1, source_target_pairs={{0,256},{16,272},{32,288},{48,304},{64,320},{80,336},{96,352},{112... | collective-permute-start | bytes 98312 | tf_op jit(solution)/shard_map/ppermute | solution.py:484
  10.2 4.3 %collective-permute-start = (f32[64,128]{1,0:T(8,128)S(1)}, f32[64,128]{1,0:T(8,128)S(1)}, u32[]{:S(2)}, u32[]{:S(2)}) collective-permute-start(f32[64,128]{1,0:T(8,128)S(1)} %get-tuple-element.22.refs_0_.refs_2_), channel_id=1, source_target_pairs={{0,496},{16,32},{32,16},{48,64},{64,48},{80,96},{96,80},{112,128},... | collective-permute-start | bytes 98312 | tf_op jit(solution)/shard_map/ppermute | solution.py:485
  14.4 3.6 %all-gather = f32[128,128]{1,0:T(8,128)S(1)} all-gather(f32[64,128]{1,0:T(8,128)S(1)} %get-tuple-element.22.refs_0_.refs_2_), channel_id=2, replica_groups={{0,16},{32,48},{64,80},{96,112},{128,144},{160,176},{192,208},{224,240}..., dimensions={0}, use_global_device_ids=true | all-gather | bytes 98304 | tf_op jit(solution)/shard_map/all_gather | solution.py:486
  18.1 0.0 collective-permute-done.1.refs_3_
  18.1 0.1 collective-permute-done.refs_2_
  18.1 3.0 %baselines.1 = (f32[32,128]{1,0:T(8,128)S(1)}, f32[4,32,128]{2,1,0:T(8,128)}) custom-call(f32[64,128]{1,0:T(8,128)S(1)} %get-tuple-element.22.refs_0_.refs_2_, f32[2,64,128]{2,1,0:T(8,128)S(1)} %bitcast.20, f32[64,128]{1,0:T(8,128)S(1)} %collective-permute-done.refs_2_, f32[64,128]{1,0:T(8,128)S(1)} %collective-permute-done.1.refs_3_, ...), custom_call_target="tpu_custom_call" | custom-call | tf_op jit(solution)/shard_map/baselines/pallas_call | solution.py:488
  21.2 6.7 %all-to-all-start = ((f32[4,32,128]{2,1,0:T(8,128)}), f32[4,32,128]{2,1,0:T(8,128)S(1)}, u32[]{:S(2)}, u32[]{:S(2)}) async-start(f32[4,32,128]{2,1,0:T(8,128)} %get-tuple-element.27), calls=%async_computation | async-start | bytes 131072 | tf_op jit(solution)/shard_map/all_to_all | solution.py:476
  27.9 0.0 copy-start
  27.9 0.0 copy-start.1
  27.9 3.4 %all-gather.1 = f32[64,128]{1,0:T(8,128)S(1)} all-gather(f32[32,128]{1,0:T(8,128)S(1)} %get-tuple-element.26), channel_id=3, replica_groups={{0,16},{32,48},{64,80},{96,112},{128,144},{160,176},{192,208},{224,240}..., dimensions={0}, use_global_device_ids=true | all-gather | bytes 49152 | tf_op jit(solution)/shard_map/all_gather | solution.py:479
  31.3 0.9 %all-to-all-done.refs_1_ = f32[4,32,128]{2,1,0:T(8,128)S(1)} async-done(((f32[4,32,128]{2,1,0:T(8,128)}), f32[4,32,128]{2,1,0:T(8,128)S(1)}, u32[]{:S(2)}, u32[]{:S(2)}) %all-to-all-start) | async-done | bytes 65568 | tf_op jit(solution)/shard_map/all_to_all | solution.py:476
  32.2 0.0 copy-done
  32.2 0.0 copy-done.1
  32.2 0.2 curvature.1
  32.4 20.4 %all_to_all.28 = f32[32,1,128]{2,1,0:T(1,128)S(1)} all-to-all(f32[32,1,128]{2,1,0:T(1,128)S(1)} %bitcast.25), channel_id=1, replica_groups=mesh['y'=8,'x'=4,'z'=8,'core'=2] {'x','z'}, dimensions={0} | all-to-all | bytes 32768 | tf_op jit(solution)/shard_map/all_to_all | solution.py:512
  52.8 0.1 line_sums.1
  52.9 0.0 copy-start.2
  52.9 15.1 %all_to_all.29 = f32[16,1,128]{2,1,0:T(1,128)S(1)} all-to-all(f32[16,1,128]{2,1,0:T(1,128)S(1)} %bitcast.24), channel_id=1, replica_groups=mesh['y'=8,'x'=4,'z'=8,'core'=2] {'y','core'}, dimensions={0} | all-to-all | bytes 16384 | tf_op jit(solution)/shard_map/all_to_all | solution.py:521
  67.9 0.0 copy-done.2
  67.9 0.8 %update.1 = (f32[4,8,128]{2,1,0:T(8,128)}, f32[2,4]{1,0:T(2,128)}, f32[4,8,128]{2,1,0:T(8,128)}, f32[2,4]{1,0:T(2,128)}, f32[4,8,128]{2,1,0:T(8,128)}, /*index=5*/f32[2,4]{1,0:T(2,128)}) custom-call(f32[16,128]{1,0:T(8,128)S(1)} %bitcast.23, f32[4,8,128]{2,1,0:T(8,128)S(1)} %get-tuple-element.31.refs_1_, f32[3,2,4]{2,1,0:T(2,128)S(1)} %get-tuple-element.29.refs_4_.refs_2_, ...), custom_call_target="tpu_custom_call" | custom-call | tf_op jit(solution)/shard_map/update/pallas_call | solution.py:523
Async XLA Ops:
  1.9 16.2 %collective-permute-start.1 = (f32[64,128]{1,0:T(8,128)S(1)}, f32[64,128]{1,0:T(8,128)S(1)}, u32[]{:S(2)}, u32[]{:S(2)}) collective-permute-start(f32[64,128]{1,0:T(8,128)S(1)} %get-tuple-element.22.refs_0_.refs_2_), channel_id=1, source_target_pairs={{0,256},{16,272},{32,288},{48,304},{64,320},{80,336},{96,352},{112... | collective-permute-start | bytes 98312 | tf_op jit(solution)/shard_map/ppermute | solution.py:484
  10.2 8.0 %collective-permute-start = (f32[64,128]{1,0:T(8,128)S(1)}, f32[64,128]{1,0:T(8,128)S(1)}, u32[]{:S(2)}, u32[]{:S(2)}) collective-permute-start(f32[64,128]{1,0:T(8,128)S(1)} %get-tuple-element.22.refs_0_.refs_2_), channel_id=1, source_target_pairs={{0,496},{16,32},{32,16},{48,64},{64,48},{80,96},{96,80},{112,128},... | collective-permute-start | bytes 98312 | tf_op jit(solution)/shard_map/ppermute | solution.py:485
  21.2 11.0 %all-to-all-start = ((f32[4,32,128]{2,1,0:T(8,128)}), f32[4,32,128]{2,1,0:T(8,128)S(1)}, u32[]{:S(2)}, u32[]{:S(2)}) async-start(f32[4,32,128]{2,1,0:T(8,128)} %get-tuple-element.27), calls=%async_computation | async-start | bytes 131072 | tf_op jit(solution)/shard_map/all_to_all | solution.py:476
  27.9 4.3 %copy-start = (f32[4,8,128]{2,1,0:T(8,128)S(1)}, f32[4,8,128]{2,1,0:T(8,128)}, u32[]{:S(2)}) copy-start(f32[4,8,128]{2,1,0:T(8,128)} %refs_3_.1) | copy-start | bytes 49156
  27.9 4.3 %copy-start.1 = (f32[4,8,128]{2,1,0:T(8,128)S(1)}, f32[4,8,128]{2,1,0:T(8,128)}, u32[]{:S(2)}) copy-start(f32[4,8,128]{2,1,0:T(8,128)} %refs_4_.1) | copy-start | bytes 49156
  52.9 15.1 %copy-start.2 = (f32[4,8,128]{2,1,0:T(8,128)S(1)}, f32[4,8,128]{2,1,0:T(8,128)}, u32[]{:S(2)}) copy-start(f32[4,8,128]{2,1,0:T(8,128)} %refs_5_.3) | copy-start | bytes 49156

commit v8 on v5

--- a/solution.py
+++ b/solution.py
@@ -314,16 +314,18 @@
             j = 2 * r + a
             curv_ref[:, j, :] = band_re[rows, :] + damping_weight * band_ref[:, j, :]
             curv_ref[:, 4 + j, :] = band_im[rows, :] + damping_weight * band_ref[:, 4 + j, :]
-    moved = jnp.sum(moved * (full_turn * delay_scale * freq), axis=1, keepdims=True)
+    moved = moved * (full_turn * delay_scale * freq)
     curv, band, res = curv_ref[...], band_ref[...], res_ref[...]
     scalars = [
-        jnp.sum(jnp.sum(jnp.sum(x, axis=0), axis=0, keepdims=True), axis=1, keepdims=True)
+        jnp.sum(jnp.sum(x, axis=0), axis=0, keepdims=True)
         for x in (res * res, res * curv, curv * curv, band * curv)
     ]
+    sums = jnp.sum(
+        jnp.concatenate([moved] + scalars + [jnp.zeros((4, width), f32)], axis=0), axis=1, keepdims=True
+    )
     here = jnp.where(lax.axis_index("z") == 0, 1.0, 0.0)
     values = jnp.concatenate(
-        [moved] + scalars + [jnp.zeros((4, 1), f32)]
-        + [here * column(small_ref.at[0]), here * column(small_ref.at[1])],
+        [sums] + [here * column(small_ref.at[0]), here * column(small_ref.at[1])],
         axis=0,
     )
     count = values.shape[0]
@@ -371,13 +373,18 @@
         lax.broadcasted_iota(jnp.int32, (count, width), 1) % part < half
     )
 
-    def delays(x):
-        return scalar(jnp.sum(jnp.where(valid, x, 0.0), axis=0, keepdims=True))
-
-    squares = scalar(jnp.where(lane == half, sums, 0.0)) + delays(lefts * lefts)
-    cross = scalar(jnp.where(lane == half + 1, sums, 0.0)) + delays(lefts * curves)
-    norm = scalar(jnp.where(lane == half + 2, sums, 0.0)) + delays(curves * curves)
-    curvature = scalar(jnp.where(lane == half + 3, sums, 0.0)) + delays(moves * curves)
+    products = (lefts * lefts, lefts * curves, curves * curves, moves * curves)
+    totals = scalar(
+        jnp.concatenate(
+            [
+                jnp.where(lane == half + k, sums, 0.0)
+                + jnp.sum(jnp.where(valid, x, 0.0), axis=0, keepdims=True)
+                for k, x in enumerate(products)
+            ],
+            axis=0,
+        )
+    )
+    squares, cross, norm, curvature = (totals[k : k + 1] for k in range(4))
     alpha = squares / curvature
     fresh = squares + alpha * (alpha * norm - 2.0 * cross)
     ratio = fresh / squares

time: 69.3 us -> 69.3 us (level)
  no operation moved by 1% of the time
where the time goes in v8:
time: 69.3 us; the launch traced here: 68.9 us
  blocking collectives  42.5 us (61%)
  starting transfers between devices  19.3 us (28%)
  Pallas kernels  5.5 us (8%)
  waiting for transfers between devices  0.96 us (1%)
    all_to_all x1, blocking collectives, body(): row = lax.all_to_all(row, ('x', 'z'), 0, 0, tiled=True)  20.4 us
    all_to_all x1, blocking collectives, body(): everyone = lax.all_to_all(row, ('y', 'core'), 0, 0, tiled=True)  15.1 us
    ppermute x1, starting transfers between devices, body(): from_far = lax.ppermute(terms, base, far_pairs)  8.28 us
    all_to_all x1, starting transfers between devices, exchange(): lax.all_to_all(to_group.reshape(4 * count, width), base, 0, 0, axis_index...  6.73 us
    ppermute x1, starting transfers between devices, body(): from_odd = lax.ppermute(terms, base, odd_pairs)  4.27 us
    all_gather x1, blocking collectives, body(): from_even = lax.all_gather(terms, base, axis_index_groups=even_groups)  3.63 us
    all_gather x1, blocking collectives, exchange(): even = lax.all_gather(to_even, base, axis_index_groups=even_groups)  3.38 us
    pallas_call x1, Pallas kernels, body(): pl.pallas_call(lambda *refs: baseline_kernel(*refs, factor=factor, blocks...  3.14 us
  transfers between devices with their start and end apart: 3, of which 2 were waited for; matrix products, arithmetic and copies ran while one was open for 0% of the time, Pallas kernels for 0%

profile of v8, /device:TPU:1, one launch (start us, length us, event | category | flops | bytes accessed | tf_op | source)
XLA Modules:
  0.0 68.9 jit_solution(247828018697570066)
XLA Ops:
  0.6 1.2 %station_terms.1 = (f32[64,128]{1,0:T(8,128)S(1)}, f32[16,128]{1,0:T(8,128)S(1)}, f32[3,2,4]{2,1,0:T(2,128)S(1)}, bf16[512,128]{1,0:T(8,128)(2,1)S(1)}, bf16[16,...) custom-call(f32[4,8,128]{2,1,0:T(8,128)} %refs_0_.1, f32[4,8,128]{2,1,0:T(8,128)} %refs_3_.1, f32[2,4]{1,0:T(2,128)} %bitcast.27, ...), custom_call_target="tpu_custom_call" | custom-call | tf_op jit(solution)/shard_map/station_terms/pallas_call | solution.py:439
  1.9 8.3 %collective-permute-start.1 = (f32[64,128]{1,0:T(8,128)S(1)}, f32[64,128]{1,0:T(8,128)S(1)}, u32[]{:S(2)}, u32[]{:S(2)}) collective-permute-start(f32[64,128]{1,0:T(8,128)S(1)} %get-tuple-element.22.refs_0_.refs_2_), channel_id=1, source_target_pairs={{0,256},{16,272},{32,288},{48,304},{64,320},{80,336},{96,352},{112... | collective-permute-start | bytes 98312 | tf_op jit(solution)/shard_map/ppermute | solution.py:485
  10.2 4.3 %collective-permute-start = (f32[64,128]{1,0:T(8,128)S(1)}, f32[64,128]{1,0:T(8,128)S(1)}, u32[]{:S(2)}, u32[]{:S(2)}) collective-permute-start(f32[64,128]{1,0:T(8,128)S(1)} %get-tuple-element.22.refs_0_.refs_2_), channel_id=1, source_target_pairs={{0,496},{16,32},{32,16},{48,64},{64,48},{80,96},{96,80},{112,128},... | collective-permute-start | bytes 98312 | tf_op jit(solution)/shard_map/ppermute | solution.py:486
  14.4 3.6 %all-gather = f32[128,128]{1,0:T(8,128)S(1)} all-gather(f32[64,128]{1,0:T(8,128)S(1)} %get-tuple-element.22.refs_0_.refs_2_), channel_id=2, replica_groups={{0,16},{32,48},{64,80},{96,112},{128,144},{160,176},{192,208},{224,240}..., dimensions={0}, use_global_device_ids=true | all-gather | bytes 98304 | tf_op jit(solution)/shard_map/all_gather | solution.py:487
  18.1 0.0 collective-permute-done.1.refs_3_
  18.1 0.1 collective-permute-done.refs_2_
  18.1 3.1 %baselines.1 = (f32[32,128]{1,0:T(8,128)S(1)}, f32[4,32,128]{2,1,0:T(8,128)}) custom-call(f32[64,128]{1,0:T(8,128)S(1)} %get-tuple-element.22.refs_0_.refs_2_, f32[2,64,128]{2,1,0:T(8,128)S(1)} %bitcast.20, f32[64,128]{1,0:T(8,128)S(1)} %collective-permute-done.refs_2_, f32[64,128]{1,0:T(8,128)S(1)} %collective-permute-done.1.refs_3_, ...), custom_call_target="tpu_custom_call" | custom-call | tf_op jit(solution)/shard_map/baselines/pallas_call | solution.py:489
  21.3 6.7 %all-to-all-start = ((f32[4,32,128]{2,1,0:T(8,128)}), f32[4,32,128]{2,1,0:T(8,128)S(1)}, u32[]{:S(2)}, u32[]{:S(2)}) async-start(f32[4,32,128]{2,1,0:T(8,128)} %get-tuple-element.27), calls=%async_computation | async-start | bytes 131072 | tf_op jit(solution)/shard_map/all_to_all | solution.py:477
  28.0 0.0 copy-start
  28.0 0.0 copy-start.1
  28.0 3.4 %all-gather.1 = f32[64,128]{1,0:T(8,128)S(1)} all-gather(f32[32,128]{1,0:T(8,128)S(1)} %get-tuple-element.26), channel_id=3, replica_groups={{0,16},{32,48},{64,80},{96,112},{128,144},{160,176},{192,208},{224,240}..., dimensions={0}, use_global_device_ids=true | all-gather | bytes 49152 | tf_op jit(solution)/shard_map/all_gather | solution.py:480
  31.4 0.9 %all-to-all-done.refs_1_ = f32[4,32,128]{2,1,0:T(8,128)S(1)} async-done(((f32[4,32,128]{2,1,0:T(8,128)}), f32[4,32,128]{2,1,0:T(8,128)S(1)}, u32[]{:S(2)}, u32[]{:S(2)}) %all-to-all-start) | async-done | bytes 65568 | tf_op jit(solution)/shard_map/all_to_all | solution.py:477
  32.3 0.0 copy-done
  32.3 0.0 copy-done.1
  32.3 0.2 curvature.1
  32.5 20.4 %all_to_all.28 = f32[32,1,128]{2,1,0:T(1,128)S(1)} all-to-all(f32[32,1,128]{2,1,0:T(1,128)S(1)} %bitcast.25), channel_id=1, replica_groups=mesh['y'=8,'x'=4,'z'=8,'core'=2] {'x','z'}, dimensions={0} | all-to-all | bytes 32768 | tf_op jit(solution)/shard_map/all_to_all | solution.py:513
  52.9 0.1 line_sums.1
  53.0 0.0 copy-start.2
  53.0 15.1 %all_to_all.29 = f32[16,1,128]{2,1,0:T(1,128)S(1)} all-to-all(f32[16,1,128]{2,1,0:T(1,128)S(1)} %bitcast.24), channel_id=1, replica_groups=mesh['y'=8,'x'=4,'z'=8,'core'=2] {'y','core'}, dimensions={0} | all-to-all | bytes 16384 | tf_op jit(solution)/shard_map/all_to_all | solution.py:522
  68.1 0.0 copy-done.2
  68.1 0.8 %update.1 = (f32[4,8,128]{2,1,0:T(8,128)}, f32[2,4]{1,0:T(2,128)}, f32[4,8,128]{2,1,0:T(8,128)}, f32[2,4]{1,0:T(2,128)}, f32[4,8,128]{2,1,0:T(8,128)}, /*index=5*/f32[2,4]{1,0:T(2,128)}) custom-call(f32[16,128]{1,0:T(8,128)S(1)} %bitcast.23, f32[4,8,128]{2,1,0:T(8,128)S(1)} %get-tuple-element.31.refs_1_, f32[3,2,4]{2,1,0:T(2,128)S(1)} %get-tuple-element.29.refs_4_.refs_2_, ...), custom_call_target="tpu_custom_call" | custom-call | tf_op jit(solution)/shard_map/update/pallas_call | solution.py:524
Async XLA Ops:
  1.9 16.2 %collective-permute-start.1 = (f32[64,128]{1,0:T(8,128)S(1)}, f32[64,128]{1,0:T(8,128)S(1)}, u32[]{:S(2)}, u32[]{:S(2)}) collective-permute-start(f32[64,128]{1,0:T(8,128)S(1)} %get-tuple-element.22.refs_0_.refs_2_), channel_id=1, source_target_pairs={{0,256},{16,272},{32,288},{48,304},{64,320},{80,336},{96,352},{112... | collective-permute-start | bytes 98312 | tf_op jit(solution)/shard_map/ppermute | solution.py:485
  10.2 8.0 %collective-permute-start = (f32[64,128]{1,0:T(8,128)S(1)}, f32[64,128]{1,0:T(8,128)S(1)}, u32[]{:S(2)}, u32[]{:S(2)}) collective-permute-start(f32[64,128]{1,0:T(8,128)S(1)} %get-tuple-element.22.refs_0_.refs_2_), channel_id=1, source_target_pairs={{0,496},{16,32},{32,16},{48,64},{64,48},{80,96},{96,80},{112,128},... | collective-permute-start | bytes 98312 | tf_op jit(solution)/shard_map/ppermute | solution.py:486
  21.3 11.0 %all-to-all-start = ((f32[4,32,128]{2,1,0:T(8,128)}), f32[4,32,128]{2,1,0:T(8,128)S(1)}, u32[]{:S(2)}, u32[]{:S(2)}) async-start(f32[4,32,128]{2,1,0:T(8,128)} %get-tuple-element.27), calls=%async_computation | async-start | bytes 131072 | tf_op jit(solution)/shard_map/all_to_all | solution.py:477
  28.0 4.3 %copy-start = (f32[4,8,128]{2,1,0:T(8,128)S(1)}, f32[4,8,128]{2,1,0:T(8,128)}, u32[]{:S(2)}) copy-start(f32[4,8,128]{2,1,0:T(8,128)} %refs_3_.1) | copy-start | bytes 49156
  28.0 4.3 %copy-start.1 = (f32[4,8,128]{2,1,0:T(8,128)S(1)}, f32[4,8,128]{2,1,0:T(8,128)}, u32[]{:S(2)}) copy-start(f32[4,8,128]{2,1,0:T(8,128)} %refs_4_.1) | copy-start | bytes 49156
  53.0 15.1 %copy-start.2 = (f32[4,8,128]{2,1,0:T(8,128)S(1)}, f32[4,8,128]{2,1,0:T(8,128)}, u32[]{:S(2)}) copy-start(f32[4,8,128]{2,1,0:T(8,128)} %refs_5_.3) | copy-start | bytes 49156
